TPU v7x, 32 devices: a whole 2x2x4 slice. The times are simulated.
32 devices in a mesh: item: 8 (over y, x, core), code: 4 (over z).
Axes of the slice: x: 2, y: 2, z: 4, core: 2. Of those that a mesh axis runs over, the one named last changes fastest.
Arguments:
- embeddings: bfloat16 [512, 65536], P('code', 'item'), may hold values from -6 to 6
- first_codes: int32 [65536], P('item'), may hold values from 0 to 8191
- second_codes: int32 [65536], P('item'), may hold values from 0 to 8191
- first_old: float32 [512, 8192], P('code', 'item'), may hold values from -6 to 6
- second_old: float32 [512, 8192], P('code', 'item'), may hold values from -3 to 3
Outputs:
- first_new: float32 [512, 8192], P('code', 'item')
- second_new: float32 [512, 8192], P('code', 'item')
- leftover: float32 [512, 65536], P('code', 'item')
All inputs are finite; a program needn't handle non-finite values.
Results may differ from a plain program's by a relative error of at most 0.0003.
Values sent between devices are 32-bit elements; how exact they have to be, the bound alone decides.
A program may use at most 64 MiB of HBM per device.

v0:
```python
import jax
import jax.numpy as jnp
from jax import lax
from jax.sharding import PartitionSpec as P

D = 512
K = 8192


def level_update(columns, codes, old):
    sums = jax.ops.segment_sum(columns.T, codes, num_segments=K).T
    counts = jax.ops.segment_sum(jnp.ones(codes.shape, jnp.float32), codes, num_segments=K)[None, :]
    own_sums, own_counts = (
        lax.psum_scatter(sums, "item", scatter_dimension=1, tiled=True),
        lax.psum_scatter(counts, "item", scatter_dimension=1, tiled=True),
    )
    own_new = 0.5 * old + 0.5 * own_sums / (own_counts + 1.0)
    whole_new = lax.all_gather(own_new, "item", axis=1, tiled=True)
    return (own_new, whole_new)


def on_device(embeddings, first_codes, second_codes, first_old, second_old):
    values = embeddings.astype(jnp.float32)
    squares = lax.psum(jnp.sum(values * values, axis=0), "code")
    normed = values * lax.rsqrt(squares / D + 1e-06)[None, :]
    first_new, first_whole = level_update(normed, first_codes, first_old)
    middle = normed - jnp.take(first_whole, first_codes, axis=1)
    second_new, second_whole = level_update(middle, second_codes, second_old)
    leftover = middle - jnp.take(second_whole, second_codes, axis=1)
    return (first_new, second_new, leftover)


def solution(mesh):
    in_specs = (P("code", "item"), P("item"), P("item"), P("code", "item"), P("code", "item"))
    out_specs = (P("code", "item"), P("code", "item"), P("code", "item"))
    return jax.shard_map(
        on_device, mesh=mesh, in_specs=in_specs, out_specs=out_specs, check_vma=False
    )
```

profile of v0, /device:TPU:1, one launch (start us, length us, event | category | flops | bytes accessed | tf_op | source)
XLA Modules:
  0.0 446.2 jit_solution(11927067216066145926)
XLA Ops:
  7.2 0.0 reduce-scatter.13.cloned.1.call-start
  7.2 43.4 %scatter_custom_fusion.1 = f32[8192]{0:T(1024)S(1)} fusion(s32[8192]{0:T(1024)} %param.8, f32[8192]{0:T(1024)S(1)} %broadcast.25, f32[]{:T(128)} %constant.1.clone.1), kind=kCustom, calls=%fused_computation.34 | custom fusion | flops 8192 | bytes 33280 | tf_op jit(solution)/shard_map/scatter-add | solution.py:12
  50.6 2.6 copy.20
  53.2 0.0 reduce-scatter.13.cloned.1.call-update
  53.3 0.0 copy-start.2
  53.3 0.0 reduce-scatter.9.cloned.1.call-start
  53.3 3.2 copy.15
  56.6 1.2 fusion.4
  57.7 16.3 %psum.7 = f32[8192]{0:T(1024)S(1)} all-reduce(f32[8192]{0:T(1024)S(1)} %fusion.4), channel_id=1, replica_groups=mesh['item'=8,'code'=4] {'code'}, use_global_device_ids=true, to_apply=%region_1.0 | all-reduce | flops 8192 | bytes 65536 | tf_op jit(solution)/shard_map/psum | solution.py:24
  74.1 0.0 copy-done.2
  74.1 0.0 copy-start.1
  74.1 50.3 %scatter_custom_fusion = f32[8192,128]{1,0:T(8,128)} fusion(s32[8192]{0:T(1024)S(1)} %copy-done.2, bf16[128,8192]{0,1:T(8,128)(2,1)S(1)} %copy.15, f32[8192]{0:T(1024)S(1)} %add_rsqrt_fusion, f32[]{:T(128)} %constant.1.clone.1), kind=kCustom, calls=%fused_computation.10 | custom fusion | flops 3145728 | bytes 6324228 | tf_op jit(solution)/shard_map/scatter-add | solution.py:11
  124.4 0.0 copy-start.3
  124.4 0.0 reduce-scatter.9.cloned.1.call-update
  124.4 0.0 all-gather.3.cloned.1.call-start
  124.5 0.0 copy-done.1
  124.5 0.2 copy.14
  124.7 0.0 reduce-scatter.13.cloned.1.call-done
  124.7 1.1 add_bitcast_fusion.1
  125.8 0.2 copy.24
  126.0 52.1 %reduce-scatter.9.cloned.1.call-done = f32[128,1024]{0,1:T(8,128)} async-done(((f32[128,8192]{0,1:T(8,128)}), f32[128,1024]{0,1:T(8,128)}) %reduce-scatter.9.cloned.1.call-update) | async-done | bytes 524304 | tf_op jit(solution)/shard_map/reduce_scatter | solution.py:14
  178.1 2.0 divide_add_fusion.1
  180.1 0.0 all-gather.3.cloned.1.call-update
  180.1 0.0 reduce-scatter.15.cloned.1.call-start
  180.2 0.0 copy-done.3
  180.2 43.2 %scatter_custom_fusion.3 = f32[8192]{0:T(1024)S(1)} fusion(s32[8192]{0:T(1024)S(1)} %copy-done.3, f32[8192]{0:T(1024)S(1)} %broadcast.25, f32[]{:T(128)} %constant.1.clone.1), kind=kCustom, calls=%fused_computation.32 | custom fusion | flops 8192 | bytes 32772 | tf_op jit(solution)/shard_map/scatter-add | solution.py:12
  223.4 2.6 copy.22
  226.0 0.0 reduce-scatter.15.cloned.1.call-update
  226.1 0.0 reduce-scatter.11.cloned.1.call-start
  226.2 0.0 all-gather.3.cloned.1.call-done
  226.2 30.1 %gather_fusion = f32[8192,128]{1,0:T(8,128)} fusion(f32[128,8192]{0,1:T(8,128)} %all-gather.3.cloned.1.call-done, s32[8192]{0:T(1024)S(1)} %fusion.14), kind=kCustom, calls=%fused_computation.clone | custom fusion | bytes 8421376 | tf_op jit(solution)/shard_map/jit(_take)/gather | solution.py:27
  256.3 47.8 %scatter_custom_fusion.2 = f32[8192,128]{1,0:T(8,128)} fusion(s32[8192]{0:T(1024)S(1)} %copy-done.3, bf16[128,8192]{0,1:T(8,128)(2,1)S(1)} %copy.15, f32[8192,128]{1,0:T(8,128)} %gather_fusion, f32[]{:T(128)} %constant.12.clone.2, f32[8192]{0:T(1024)S(1)} %add_rsqrt_fusion, f32[]{:T(128)} %constant.1.clone.1, pred[8192]{0:T(1024)(128)(4,1)S(1)} %compare_and_fusion.1), kind=kCustom, calls=%fused_computation.13 | custom fusion | flops 5242880 | bytes 10526728 | tf_op jit(solution)/shard_map/scatter-add | solution.py:11
  304.1 0.0 reduce-scatter.11.cloned.1.call-update
  304.2 0.0 all-gather.5.cloned.1.call-start
  304.2 1.3 copy.16
  305.5 0.0 reduce-scatter.15.cloned.1.call-done
  305.5 1.9 add_bitcast_fusion
  307.4 1.2 copy.25
  308.6 47.0 %reduce-scatter.11.cloned.1.call-done = f32[128,1024]{0,1:T(8,128)} async-done(((f32[128,8192]{0,1:T(8,128)}), f32[128,1024]{0,1:T(8,128)}) %reduce-scatter.11.cloned.1.call-update) | async-done | bytes 524304 | tf_op jit(solution)/shard_map/reduce_scatter | solution.py:14
  355.6 2.0 divide_add_fusion
  357.7 0.0 all-gather.5.cloned.1.call-update
  357.7 0.0 copy-done
  357.8 1.0 copy.17
  358.8 2.0 copy.18
  360.8 34.2 %all-gather.5.cloned.1.call-done = f32[128,8192]{0,1:T(8,128)} async-done(((f32[128,1024]{0,1:T(8,128)}), f32[128,8192]{0,1:T(8,128)}) %all-gather.5.cloned.1.call-update) | async-done | bytes 4194320 | tf_op jit(solution)/shard_map/all_gather | solution.py:18
  395.0 29.9 %gather_fusion.1 = f32[8192,128]{1,0:T(8,128)} fusion(f32[128,8192]{0,1:T(8,128)} %all-gather.5.cloned.1.call-done, s32[8192]{0:T(1024)S(1)} %fusion.15), kind=kCustom, calls=%fused_computation.1.clone | custom fusion | bytes 8421376 | tf_op jit(solution)/shard_map/jit(_take)/gather | solution.py:29
  424.9 8.8 %bitcast_subtract_fusion = f32[128,8192]{0,1:T(8,128)} fusion(f32[8192,128]{1,0:T(8,128)} %gather_fusion.1, f32[8192,128]{1,0:T(8,128)} %gather_fusion, bf16[128,8192]{0,1:T(8,128)(2,1)S(1)} %copy.15, f32[8192]{0:T(1024)S(1)} %add_rsqrt_fusion, pred[8192]{0:T(1024)(128)(4,1)S(1)} %compare_and_fusion, pred[8192]{0:T(1024)(128)(4,1)S(1)} %compare_and_fusion.1), kind=kLoop, calls=%fused_computation.12 | loop fusion | flops 6291456 | bytes 14729216 | tf_op jit(solution)/shard_map/sub | solution.py:29
  433.7 5.6 %copy.19 = f32[128,8192]{1,0:T(8,128)} copy(f32[128,8192]{0,1:T(8,128)} %bitcast_subtract_fusion) | data formatting | bytes 8388608
  (7 shorter events, 0.1 us)
Async XLA Ops:
  7.2 117.5 %reduce-scatter.13.cloned.1.call-start = ((), (), s32[]{:S(2)}) async-start(), calls=%async_computation.8 | async-start | bytes 4718592
  53.3 20.8 %copy-start.2 = (s32[8192]{0:T(1024)S(1)}, s32[8192]{0:T(1024)}, u32[]{:S(2)}) copy-start(s32[8192]{0:T(1024)} %param.8) | copy-start | bytes 98308
  53.3 124.8 %reduce-scatter.9.cloned.1.call-start = ((), (), s32[]{:S(2)}) async-start(), calls=%async_computation.4 | async-start | bytes 4718592 | tf_op jit(solution)/shard_map/reduce_scatter | solution.py:14
  74.1 50.4 %copy-start.1 = (f32[128,1024]{1,0:T(8,128)S(1)}, f32[128,1024]{1,0:T(8,128)}, u32[]{:S(2)}) copy-start(f32[128,1024]{1,0:T(8,128)} %param.10) | copy-start | bytes 1572868
  124.4 55.8 %copy-start.3 = (s32[8192]{0:T(1024)S(1)}, s32[8192]{0:T(1024)}, u32[]{:S(2)}) copy-start(s32[8192]{0:T(1024)} %param.9) | copy-start | bytes 98308
  124.4 101.8 %all-gather.3.cloned.1.call-start = ((), (), s32[]{:S(2)}) async-start(), calls=%async_computation.5 | async-start | bytes 4718592 | tf_op jit(solution)/shard_map/all_gather | solution.py:18
  180.1 125.4 %reduce-scatter.15.cloned.1.call-start = ((), (), s32[]{:S(2)}) async-start(), calls=%async_computation.9 | async-start | bytes 4718592
  226.1 129.6 %reduce-scatter.11.cloned.1.call-start = ((), (), s32[]{:S(2)}) async-start(), calls=%async_computation.6 | async-start | bytes 4718592 | tf_op jit(solution)/shard_map/reduce_scatter | solution.py:14
  304.1 53.6 %copy-start = (f32[128,1024]{0,1:T(8,128)S(1)}, f32[128,1024]{0,1:T(8,128)}, u32[]{:S(2)}) copy-start(f32[128,1024]{0,1:T(8,128)} %divide_add_fusion.1) | copy-start | bytes 1572868
  304.2 90.8 %all-gather.5.cloned.1.call-start = ((), (), s32[]{:S(2)}) async-start(), calls=%async_computation.7 | async-start | bytes 4718592 | tf_op jit(solution)/shard_map/all_gather | solution.py:18
Sparse Core Ops, SparseCore 0:
  53.4 53.3 reduce-scatter.12
  124.5 53.4 reduce-scatter.8
  180.5 37.1 all-gather.2
  226.2 51.2 reduce-scatter.14
  304.3 51.3 reduce-scatter.10
  357.8 37.1 all-gather.4
where the time goes:
time: 447 us; the launch traced here: 446 us
  other arithmetic  202 us (45%)
  waiting for transfers between devices  133 us (30%)
  local copies, waits for them, and re-layouts  80 us (18%)
  blocking collectives  16.3 us (4%)
  between operations  14.3 us (3%)
    reduce_scatter x2, waiting for transfers between devices, level_update(): lax.psum_scatter(sums, 'item', scatter_dimension=1, tiled=True)  99.1 us
    scatter-add x2, other arithmetic, level_update(): sums = jax.ops.segment_sum(columns.T, codes, num_segments=K).T  98.1 us
    scatter-add x2, other arithmetic, level_update(): jax.ops.segment_sum(jnp.ones(codes.shape, jnp.float32), codes, num_segmen...  86.6 us
    all_gather x2, waiting for transfers between devices, level_update(): whole_new = lax.all_gather(own_new, 'item', axis=1, tiled=True)  34.2 us
    gather x1, local copies, waits for them, and re-layouts, on_device(): middle = normed - jnp.take(first_whole, first_codes, axis=1)  30.1 us
    gather x1, local copies, waits for them, and re-layouts, on_device(): leftover = middle - jnp.take(second_whole, second_codes, axis=1)  29.9 us
    unnamed x18, local copies, waits for them, and re-layouts  20 us
    psum x1, blocking collectives, on_device(): squares = lax.psum(jnp.sum(values * values, axis=0), 'code')  16.3 us
  transfers between devices with their start and end apart: 6, of which 3 were waited for; matrix products, arithmetic and copies ran while one was open for 42% of the time, Pallas kernels for 0%

commit v1 on v0

v1 whole, which is shorter than its diff:
```python
import functools
import itertools

import jax
import jax.numpy as jnp
from jax import lax
from jax.experimental import pallas as pl
from jax.experimental.pallas import tpu as pltpu
from jax.sharding import PartitionSpec as P

D = 512
LANES = 128
GROUP = 8
PILES = 4
VMEM_BYTES = 52 * 1024 * 1024

VMEM = pl.BlockSpec(memory_space=pltpu.VMEM)
SMEM = pl.BlockSpec(memory_space=pltpu.SMEM)


def flip(me, bits):
    other = me
    for bit in bits:
        weight = 2**bit
        other = other + weight - 2 * weight * lax.rem(lax.div(me, weight), 2)
    return other


def subsets(bits, choice):
    return [tuple(b for b, c in zip(bits, pick) if c) for pick in itertools.product(choice, repeat=len(bits))]


def scales_kernel(n, e_ref, scale_ref, parts, send_sems, recv_sems):
    me = lax.axis_index("code")
    barrier = pltpu.get_barrier_semaphore()
    for step in range(1, n):
        pl.semaphore_signal(barrier, inc=1, device_id={"code": lax.rem(me + step, n)}, device_id_type=pl.DeviceIdType.MESH)
    items = e_ref.shape[1]
    width = min(items, 8 * LANES)

    @pl.loop(0, items // width)
    def _(at):
        columns = pl.ds(pl.multiple_of(at * width, width), width)
        values = e_ref[:, columns].astype(jnp.float32)
        parts[0, :, columns] = jnp.sum(values * values, axis=0, keepdims=True)

    pl.semaphore_wait(barrier, n - 1)
    copies = []
    for step in range(1, n):
        copy = pltpu.make_async_remote_copy(
            src_ref=parts.at[0],
            dst_ref=parts.at[step],
            send_sem=send_sems.at[step],
            recv_sem=recv_sems.at[step],
            device_id={"code": lax.rem(me + step, n)},
            device_id_type=pl.DeviceIdType.MESH,
        )
        copy.start()
        copies.append(copy)
    for copy in copies:
        copy.wait()
    squares = parts[0]
    for step in range(1, n):
        squares = squares + parts[step]
    scale_ref[...] = lax.rsqrt(squares / D + 1e-06)


def scales_of(embeddings, n):
    items = embeddings.shape[1]
    return pl.pallas_call(
        functools.partial(scales_kernel, n),
        out_shape=jax.ShapeDtypeStruct((1, items), jnp.float32),
        in_specs=[VMEM],
        out_specs=VMEM,
        scratch_shapes=[
            pltpu.VMEM((n, 1, items), jnp.float32),
            pltpu.SemaphoreType.DMA((n,)),
            pltpu.SemaphoreType.DMA((n,)),
        ],
        compiler_params=pltpu.CompilerParams(collective_id=0, has_side_effects=True, vmem_limit_bytes=VMEM_BYTES),
        cost_estimate=pl.CostEstimate(flops=0, bytes_accessed=16 * 2**20, transcendentals=0),
        name="scales",
    )(embeddings)


def clear(piles):
    rows = piles[0].shape[0]
    step = min(rows, 256)

    @pl.loop(0, rows // step)
    def _(at):
        for pile in piles:
            pile[pl.ds(pl.multiple_of(at * step, step), step), :] = jnp.zeros((step, pile.shape[1]), pile.dtype)


def merge(piles):
    rows = piles[0].shape[0]
    step = min(rows, 256)

    @pl.loop(0, rows // step)
    def _(at):
        where = pl.ds(pl.multiple_of(at * step, step), step)
        piles[0][where, :] = (piles[0][where, :] + piles[1][where, :]) + (piles[2][where, :] + piles[3][where, :])


def add_rows(piles, codes, rows):
    held = [piles[at % PILES][pl.ds(code, 1), :] for at, code in enumerate(codes)]
    first = [held[at] + rows[at] for at in range(PILES)]
    second = [
        jnp.where(codes[at] == codes[at + PILES], first[at], held[at + PILES]) + rows[at + PILES] for at in range(PILES)
    ]
    for at in range(PILES):
        piles[at][pl.ds(codes[at], 1), :] = first[at]
    for at in range(PILES):
        piles[at][pl.ds(codes[at + PILES], 1), :] = second[at]


def first_kernel(codes_ref, e_ref, scale_ref, normed_ref, sums_ref, *more):
    piles = (sums_ref,) + more
    items = e_ref.shape[1]
    clear(piles)

    @pl.loop(0, items // LANES)
    def _(at):
        span = pl.ds(pl.multiple_of(at * LANES, LANES), LANES)
        normed_ref[span, :] = (e_ref[:, span].astype(jnp.float32) * scale_ref[:, span]).T

    @pl.loop(0, items // GROUP, unroll=2)
    def _(at):
        base = pl.multiple_of(at * GROUP, GROUP)
        rows = [normed_ref[pl.ds(base + j, 1), :] for j in range(GROUP)]
        add_rows(piles, [codes_ref[base + j] for j in range(GROUP)], rows)

    merge(piles)


def second_kernel(first_ref, second_ref, normed_ref, table_ref, middle_ref, sums_ref, *more):
    piles = (sums_ref,) + more
    items = normed_ref.shape[0]
    clear(piles)

    @pl.loop(0, items // GROUP, unroll=2)
    def _(at):
        base = pl.multiple_of(at * GROUP, GROUP)
        rows = [
            normed_ref[pl.ds(base + j, 1), :] - table_ref[pl.ds(first_ref[base + j], 1), :] for j in range(GROUP)
        ]
        add_rows(piles, [second_ref[base + j] for j in range(GROUP)], rows)
        for j in range(GROUP):
            middle_ref[pl.ds(base + j, 1), :] = rows[j]

    merge(piles)


def last_kernel(block, codes_ref, middle_ref, table_ref, out_ref, named):
    start = pl.program_id(0) * block

    @pl.loop(0, block // GROUP, unroll=2)
    def _(at):
        base = pl.multiple_of(at * GROUP, GROUP)
        rows = [table_ref[pl.ds(codes_ref[start + base + j], 1), :] for j in range(GROUP)]
        for j in range(GROUP):
            named[pl.ds(base + j, 1), :] = rows[j]

    @pl.loop(0, block // LANES)
    def _(at):
        span = pl.ds(pl.multiple_of(at * LANES, LANES), LANES)
        out_ref[:, span] = (middle_ref[span, :] - named[span, :]).T


def exchange_kernel(n, sums_ref, old_ref, inverse_ref, whole_ref, own_ref, slots, send_in, recv_in, send_out, recv_out):
    levels = n.bit_length() - 1
    me = lax.axis_index("item")
    size = sums_ref.shape[0] // n
    half = size // 2
    rest = list(range(1, levels))
    orders = ([0] + rest, [0] + rest[::-1])

    def block(owner, path):
        return pl.ds(pl.multiple_of(owner * size + path * half, half), half)

    place_in, place_out = {}, {}
    for path, order in enumerate(orders):
        for step in range(levels):
            for far in subsets(order[step + 1:], (1, 0)):
                place_in[path, step, frozenset(far)] = len(place_in)
            for held in subsets(order[::-1][:step], (0, 1)):
                place_out[path, step, frozenset(held)] = len(place_out)

    sent = []

    def send_sum(path, step, far, source):
        slot = place_in[path, step, frozenset(far)]
        copy = pltpu.make_async_remote_copy(
            src_ref=source,
            dst_ref=slots.at[slot],
            send_sem=send_in.at[slot],
            recv_sem=recv_in.at[slot],
            device_id={"item": flip(me, [orders[path][step]])},
            device_id_type=pl.DeviceIdType.MESH,
        )
        copy.start()
        sent.append(copy)

    def new_copy(path, step, held, rows):
        slot = place_out[path, step, frozenset(held)]
        return pltpu.make_async_remote_copy(
            src_ref=whole_ref.at[rows],
            dst_ref=whole_ref.at[rows],
            send_sem=send_out.at[slot],
            recv_sem=recv_out.at[slot],
            device_id={"item": flip(me, [orders[path][::-1][step]])},
            device_id_type=pl.DeviceIdType.MESH,
        )

    def send_new(path, step, held):
        copy = new_copy(path, step, held, block(flip(me, held), path))
        copy.start()
        sent.append(copy)

    barrier = pltpu.get_barrier_semaphore()
    for bit in range(levels):
        pl.semaphore_signal(barrier, inc=1, device_id={"item": flip(me, [bit])}, device_id_type=pl.DeviceIdType.MESH)
    pl.semaphore_wait(barrier, levels)

    for fars in zip(*(subsets(order[1:], (1, 0)) for order in orders)):
        for path, far in enumerate(fars):
            send_sum(path, 0, far, sums_ref.at[block(flip(me, (0,) + far), path)])
    for step in range(levels):
        for fars in zip(*(subsets(order[step + 1:], (1, 0)) for order in orders)):
            for path, far in enumerate(fars):
                slot = place_in[path, step, frozenset(far)]
                pltpu.make_async_remote_copy(
                    src_ref=slots.at[slot],
                    dst_ref=slots.at[slot],
                    send_sem=send_in.at[slot],
                    recv_sem=recv_in.at[slot],
                    device_id={"item": flip(me, [orders[path][step]])},
                    device_id_type=pl.DeviceIdType.MESH,
                ).wait_recv()
                if step == 0:
                    mine = sums_ref[block(flip(me, far), path), :]
                else:
                    mine = slots[place_in[path, step - 1, frozenset(far)]]
                total = slots[slot] + mine
                if step < levels - 1:
                    slots[slot] = total
                    ahead = orders[path][step + 1]
                    if ahead in far:
                        send_sum(path, step + 1, tuple(b for b in far if b != ahead), slots.at[slot])
                else:
                    rows = pl.ds(path * half, half)
                    new = old_ref[rows, :] + total * inverse_ref[rows, :]
                    own_ref[rows, :] = new
                    whole_ref[block(me, path), :] = new
                    for later in range(levels):
                        send_new(path, later, ())

    for step in range(levels):
        for helds in zip(*(subsets(order[::-1][:step], (0, 1)) for order in orders)):
            for path, held in enumerate(helds):
                got = held + (orders[path][::-1][step],)
                new_copy(path, step, held, block(flip(me, got), path)).wait_recv()
                for later in range(step + 1, levels):
                    send_new(path, later, got)
    for copy in sent:
        copy.wait_send()


def exchange(sums, old, inverse, n, collective_id):
    rows, width = sums.shape
    size = rows // n
    count = 2 * (n - 1)
    return pl.pallas_call(
        functools.partial(exchange_kernel, n),
        out_shape=(jax.ShapeDtypeStruct(sums.shape, jnp.float32), jax.ShapeDtypeStruct((size, width), jnp.float32)),
        in_specs=[VMEM] * 3,
        out_specs=(VMEM, VMEM),
        scratch_shapes=[
            pltpu.VMEM((count, size // 2, width), jnp.float32),
            pltpu.SemaphoreType.DMA((count,)),
            pltpu.SemaphoreType.DMA((count,)),
            pltpu.SemaphoreType.DMA((count,)),
            pltpu.SemaphoreType.DMA((count,)),
        ],
        compiler_params=pltpu.CompilerParams(
            collective_id=collective_id, has_side_effects=True, vmem_limit_bytes=VMEM_BYTES
        ),
        cost_estimate=pl.CostEstimate(flops=0, bytes_accessed=128 * 2**20, transcendentals=0),
        name="exchange",
    )(sums, old, inverse)


def counts_of(codes, total):
    high = lax.shift_right_logical(codes, 7)[None, :] == jnp.arange(total // LANES, dtype=codes.dtype)[:, None]
    low = lax.bitwise_and(codes, LANES - 1)[None, :] == jnp.arange(LANES, dtype=codes.dtype)[:, None]
    return lax.dot_general(
        high.astype(jnp.bfloat16),
        low.astype(jnp.bfloat16),
        (((1,), (1,)), ((), ())),
        preferred_element_type=jnp.float32,
    )


def on_device(owners, feature_parts, embeddings, first_codes, second_codes, first_old, second_old):
    width, items = embeddings.shape
    total = first_old.shape[1] * owners
    f32 = jnp.float32
    local = pltpu.CompilerParams(vmem_limit_bytes=VMEM_BYTES)
    cost = pl.CostEstimate(flops=0, bytes_accessed=64 * 2**20, transcendentals=0)

    counts = jnp.stack([counts_of(first_codes, total), counts_of(second_codes, total)], axis=1)
    counts = lax.psum_scatter(counts, "item", scatter_dimension=0, tiled=True)
    halves = 0.5 / (counts + 1.0)
    first_inverse, second_inverse = (
        jnp.broadcast_to(halves[:, level].reshape(-1, 1), (total // owners, width)) for level in range(2)
    )
    piles = [pltpu.VMEM((total, width), f32)] * (PILES - 1)
    row_sums = jax.ShapeDtypeStruct((total, width), f32)
    row_items = jax.ShapeDtypeStruct((items, width), f32)

    scales = scales_of(embeddings, feature_parts)
    normed, first_sums = pl.pallas_call(
        first_kernel,
        out_shape=(row_items, row_sums),
        in_specs=[SMEM, VMEM, VMEM],
        out_specs=(VMEM, VMEM),
        scratch_shapes=piles,
        compiler_params=local,
        cost_estimate=cost,
        name="first_sums",
    )(first_codes, embeddings, scales)
    first_whole, first_own = exchange(first_sums, 0.5 * first_old.T, first_inverse, owners, 1)
    middle, second_sums = pl.pallas_call(
        second_kernel,
        out_shape=(row_items, row_sums),
        in_specs=[SMEM, SMEM, VMEM, VMEM],
        out_specs=(VMEM, VMEM),
        scratch_shapes=piles,
        compiler_params=local,
        cost_estimate=cost,
        name="second_sums",
    )(first_codes, second_codes, normed, first_whole)
    second_whole, second_own = exchange(second_sums, 0.5 * second_old.T, second_inverse, owners, 2)
    block = min(items, 1024)
    leftover = pl.pallas_call(
        functools.partial(last_kernel, block),
        out_shape=jax.ShapeDtypeStruct((width, items), f32),
        grid=(items // block,),
        in_specs=[
            SMEM,
            pl.BlockSpec((block, width), lambda at: (at, 0)),
            pl.BlockSpec((total, width), lambda at: (0, 0)),
        ],
        out_specs=pl.BlockSpec((width, block), lambda at: (0, at)),
        scratch_shapes=[pltpu.VMEM((block, width), f32)],
        compiler_params=local,
        cost_estimate=cost,
        name="leftover",
    )(second_codes, middle, second_whole)
    return (first_own.T, second_own.T, leftover)


def solution(mesh):
    in_specs = (P("code", "item"), P("item"), P("item"), P("code", "item"), P("code", "item"))
    out_specs = (P("code", "item"), P("code", "item"), P("code", "item"))
    return jax.shard_map(
        functools.partial(on_device, mesh.shape["item"], mesh.shape["code"]),
        mesh=mesh,
        in_specs=in_specs,
        out_specs=out_specs,
        check_vma=False,
    )
```

time: 447 us -> 200 us (0.45)
  other arithmetic: 202 us -> 3.02 us
  Pallas kernels: 0 us -> 178 us
  waiting for transfers between devices: 133 us -> 0.02 us
  local copies, waits for them, and re-layouts: 80 us -> 2.78 us
  blocking collectives: 16.3 us -> 0 us
    scatter-add x4 -> x0, other arithmetic: 185 us -> none  [the longest x2 98.1 us: level_update(): sums = jax.ops.segment_sum(columns.T, codes, num_segments=K).T]
    pallas_call x0 -> x6, Pallas kernels: none -> 178 us  [the longest x2 97 us: exchange(): pl.pallas_call(functools.partial(exchange_kernel, n), out_shape=(jax.Shap...]
    reduce_scatter x2 -> x1, waiting for transfers between devices: 99.1 us -> 0.01 us  [on_device(): counts = lax.psum_scatter(counts, 'item', scatter_dimension=0, tiled=True)]
    gather x2 -> x0, local copies, waits for them, and re-layouts: 60.1 us -> none  [the longest x1 30.1 us: on_device(): middle = normed - jnp.take(first_whole, first_codes, axis=1)]
    all_gather x2 -> x0, waiting for transfers between devices: 34.2 us -> none  [level_update(): whole_new = lax.all_gather(own_new, 'item', axis=1, tiled=True)]
    unnamed x18 -> x12, local copies, waits for them, and re-layouts: 20 us -> 2.39 us
    psum x1 -> x0, blocking collectives: 16.3 us -> none  [on_device(): squares = lax.psum(jnp.sum(values * values, axis=0), 'code')]
    sub x1 -> x0, other arithmetic: 8.85 us -> none  [on_device(): leftover = middle - jnp.take(second_whole, second_codes, axis=1)]
  transfers between devices with their start and end apart: 6 -> 1, of which waited for: 3 -> 0; matrix products, arithmetic and copies ran while one was open for 42% -> 0% of each run, Pallas kernels for 0% -> 18%
where the time goes in v1:
time: 200 us
  Pallas kernels  178 us (89%)
  between operations  14.2 us (7%)
  other arithmetic  3.02 us (2%)
  local copies, waits for them, and re-layouts  2.78 us (1%)
  matrix products  2.04 us (1%)
    pallas_call x2, Pallas kernels, exchange(): pl.pallas_call(functools.partial(exchange_kernel, n), out_shape=(jax.Shap...  97 us
    pallas_call x1, Pallas kernels, on_device(): pl.pallas_call(first_kernel, out_shape=(row_items, row_sums), in_specs=[S...  26.8 us
    pallas_call x1, Pallas kernels, on_device(): pl.pallas_call(second_kernel, out_shape=(row_items, row_sums), in_specs=[...  26.6 us
    pallas_call x1, Pallas kernels, on_device(): pl.pallas_call(functools.partial(last_kernel, block), out_shape=jax.Shape...  18.8 us
    pallas_call x1, Pallas kernels, scales_of(): pl.pallas_call(functools.partial(scales_kernel, n), out_shape=jax.ShapeDt...  8.4 us
  transfers between devices with their start and end apart: 1, of which 0 were waited for; matrix products, arithmetic and copies ran while one was open for 0% of the time, Pallas kernels for 18%

profile of v1, /device:TPU:1, one launch (start us, length us, event | category | flops | bytes accessed | tf_op | source)
XLA Modules:
  0.0 199.7 jit_solution(13906087012538382847)
XLA Ops:
  7.2 0.0 copy-start.2
  7.2 0.0 copy-start.3
  7.2 0.0 reduce-scatter.2.cloned.1.call-start
  7.2 0.8 broadcast_shift-right-logical_fusion
  8.1 0.8 broadcast_shift-right-logical_fusion.1
  8.8 1.0 fusion.4
  9.9 0.0 copy-start
  9.9 1.0 fusion.5
  10.9 0.6 pad_maximum_fusion
  11.5 0.0 reduce-scatter.2.cloned.1.call-update
  11.6 0.0 copy-done.2
  11.6 0.2 copy.8
  11.8 0.0 copy-done.3
  11.8 0.2 copy.9
  12.1 8.4 %scales.1.scale_ref = f32[1,8192]{1,0:T(1,128)S(1)} custom-call(bf16[128,8192]{1,0:T(8,128)(2,1)} %e_ref.3), custom_call_target="tpu_custom_call" | custom-call | bytes 16777216 | tf_op jit(solution)/shard_map/scales/pallas_call | solution.py:70
  20.5 0.0 copy-done
  20.5 0.0 copy-start.1
  20.5 26.8 %first_sums.1 = (f32[8192,128]{1,0:T(8,128)}, f32[8192,128]{1,0:T(8,128)}) custom-call(s32[8192]{0:T(1024)S(1)} %copy-done, bf16[128,8192]{1,0:T(8,128)(2,1)} %e_ref.3, f32[1,8192]{1,0:T(1,128)S(1)} %scales.1.scale_ref), custom_call_target="tpu_custom_call" | custom-call | bytes 67108864 | tf_op jit(solution)/shard_map/first_sums/pallas_call | solution.py:323
  47.3 0.0 reduce-scatter.2.cloned.1.call-done
  47.3 0.7 add_divide_fusion
  48.0 0.2 broadcast_in_dim.9.inverse_ref
  48.2 49.9 %exchange.2 = (f32[8192,128]{1,0:T(8,128)}, f32[1024,128]{1,0:T(8,128)S(1)}) custom-call(f32[8192,128]{1,0:T(8,128)} %get-tuple-element.11.sums_ref, f32[1024,128]{1,0:T(8,128)S(1)} %multiply_bitcast_fusion.1.old_ref, f32[1024,128]{1,0:T(8,128)S(1)} %broadcast_in_dim.9.inverse_ref), custom_call_target="tpu_custom_call" | custom-call | bytes 134217728 | tf_op jit(solution)/shard_map/exchange/pallas_call | solution.py:274
  98.1 1.0 copy.10
  99.1 0.0 copy-done.1
  99.1 26.6 %second_sums.1 = (f32[8192,128]{1,0:T(8,128)}, f32[8192,128]{1,0:T(8,128)}) custom-call(s32[8192]{0:T(1024)S(1)} %copy-done, s32[8192]{0:T(1024)S(1)} %copy-done.1, f32[8192,128]{1,0:T(8,128)} %get-tuple-element.13.normed_ref, f32[8192,128]{1,0:T(8,128)} %get-tuple-element.14.table_ref), custom_call_target="tpu_custom_call" | custom-call | bytes 67108864 | tf_op jit(solution)/shard_map/second_sums/pallas_call | solution.py:334
  125.7 0.2 broadcast_in_dim.11.inverse_ref
  125.9 47.1 %exchange.3 = (f32[8192,128]{1,0:T(8,128)}, f32[1024,128]{1,0:T(8,128)S(1)}) custom-call(f32[8192,128]{1,0:T(8,128)} %get-tuple-element.15.sums_ref, f32[1024,128]{1,0:T(8,128)S(1)} %multiply_bitcast_fusion.old_ref, f32[1024,128]{1,0:T(8,128)S(1)} %broadcast_in_dim.11.inverse_ref), custom_call_target="tpu_custom_call" | custom-call | bytes 134217728 | tf_op jit(solution)/shard_map/exchange/pallas_call | solution.py:274
  173.0 1.0 copy.11
  174.0 18.8 %leftover.1 = f32[128,8192]{1,0:T(8,128)} custom-call(s32[8192]{0:T(1024)S(1)} %copy-done.1, f32[8192,128]{1,0:T(8,128)} %get-tuple-element.17.middle_ref, f32[8192,128]{1,0:T(8,128)} %get-tuple-element.18.table_ref), custom_call_target="tpu_custom_call" | custom-call | bytes 67108864 | tf_op jit(solution)/shard_map/leftover/pallas_call | solution.py:346
  (3 shorter events, 0.1 us)
Async XLA Ops:
  7.2 4.4 %copy-start.2 = (f32[128,1024]{1,0:T(8,128)S(1)}, f32[128,1024]{1,0:T(8,128)}, u32[]{:S(2)}) copy-start(f32[128,1024]{1,0:T(8,128)} %param.8) | copy-start | bytes 1572868
  7.2 4.6 %copy-start.3 = (f32[128,1024]{1,0:T(8,128)S(1)}, f32[128,1024]{1,0:T(8,128)}, u32[]{:S(2)}) copy-start(f32[128,1024]{1,0:T(8,128)} %param.9) | copy-start | bytes 1572868
  7.2 40.1 %reduce-scatter.2.cloned.1.call-start = ((), (), s32[]{:S(2)}) async-start(), calls=%async_computation.1 | async-start | bytes 73728 | tf_op jit(solution)/shard_map/reduce_scatter | solution.py:313
  9.9 10.6 %copy-start = (s32[8192]{0:T(1024)S(1)}, s32[8192]{0:T(1024)}, u32[]{:S(2)}) copy-start(s32[8192]{0:T(1024)} %first_ref.1) | copy-start | bytes 98308
  20.5 78.6 %copy-start.1 = (s32[8192]{0:T(1024)S(1)}, s32[8192]{0:T(1024)}, u32[]{:S(2)}) copy-start(s32[8192]{0:T(1024)} %codes_ref.3) | copy-start | bytes 98308
Sparse Core Ops, SparseCore 0:
  11.7 33.0 reduce-scatter.1

commit v2 on v1

--- a/solution.py
+++ b/solution.py
@@ -10,9 +10,10 @@
 
 D = 512
 LANES = 128
-GROUP = 8
-PILES = 4
-VMEM_BYTES = 52 * 1024 * 1024
+PILES = 8
+GROUP = 2 * PILES
+SPAN = 64
+MIB = 2**20
 
 VMEM = pl.BlockSpec(memory_space=pltpu.VMEM)
 SMEM = pl.BlockSpec(memory_space=pltpu.SMEM)
@@ -30,11 +31,18 @@
     return [tuple(b for b, c in zip(bits, pick) if c) for pick in itertools.product(choice, repeat=len(bits))]
 
 
-def scales_kernel(n, e_ref, scale_ref, parts, send_sems, recv_sems):
-    me = lax.axis_index("code")
+def prepare_kernel(
+    n, owners, e_ref, first_ref, second_ref, scale_ref, inverse_ref, parts, counts, got, send_sems, recv_sems,
+    send_counts, recv_counts
+):
+    me, home = lax.axis_index("code"), lax.axis_index("item")
     barrier = pltpu.get_barrier_semaphore()
     for step in range(1, n):
         pl.semaphore_signal(barrier, inc=1, device_id={"code": lax.rem(me + step, n)}, device_id_type=pl.DeviceIdType.MESH)
+    for step in range(1, owners):
+        pl.semaphore_signal(
+            barrier, inc=1, device_id={"item": lax.rem(home + step, owners)}, device_id_type=pl.DeviceIdType.MESH
+        )
     items = e_ref.shape[1]
     width = min(items, 8 * LANES)
 
@@ -44,7 +52,7 @@
         values = e_ref[:, columns].astype(jnp.float32)
         parts[0, :, columns] = jnp.sum(values * values, axis=0, keepdims=True)
 
-    pl.semaphore_wait(barrier, n - 1)
+    pl.semaphore_wait(barrier, n + owners - 2)
     copies = []
     for step in range(1, n):
         copy = pltpu.make_async_remote_copy(
@@ -57,35 +65,76 @@
         )
         copy.start()
         copies.append(copy)
-    for copy in copies:
+
+    rows = counts.shape[2]
+    high_of = lax.broadcasted_iota(jnp.int32, (owners * rows, width), 0)
+    low_of = lax.broadcasted_iota(jnp.int32, (LANES, width), 0)
+    for level, codes_ref in enumerate((first_ref, second_ref)):
+
+        def add(at, total):
+            codes = codes_ref[:, pl.ds(pl.multiple_of(at * width, width), width)]
+            high = jnp.where(lax.shift_right_logical(codes, 7) == high_of, 1.0, 0.0).astype(jnp.bfloat16)
+            low = jnp.where(lax.bitwise_and(codes, LANES - 1) == low_of, 1.0, 0.0).astype(jnp.bfloat16)
+            return total + lax.dot_general(high, low, (((1,), (1,)), ((), ())), preferred_element_type=jnp.float32)
+
+        total = lax.fori_loop(0, items // width, add, jnp.zeros((owners * rows, LANES), jnp.float32))
+        for owner in range(owners):
+            counts[owner, level] = total[owner * rows:(owner + 1) * rows]
+    for step in range(1, owners):
+        there = lax.rem(home + step, owners)
+        copy = pltpu.make_async_remote_copy(
+            src_ref=counts.at[there],
+            dst_ref=got.at[step],
+            send_sem=send_counts.at[step],
+            recv_sem=recv_counts.at[step],
+            device_id={"item": there},
+            device_id_type=pl.DeviceIdType.MESH,
+        )
+        copy.start()
+        copies.append(copy)
+    for copy in copies[:n - 1]:
         copy.wait()
     squares = parts[0]
     for step in range(1, n):
         squares = squares + parts[step]
     scale_ref[...] = lax.rsqrt(squares / D + 1e-06)
-
-
-def scales_of(embeddings, n):
+    for copy in copies[n - 1:]:
+        copy.wait()
+    held = counts[home]
+    for step in range(1, owners):
+        held = held + got[step]
+    inverse_ref[...] = 0.5 / (held + 1.0)
+
+
+def prepare(embeddings, first_codes, second_codes, n, owners, total):
     items = embeddings.shape[1]
+    rows = total // owners // LANES
     return pl.pallas_call(
-        functools.partial(scales_kernel, n),
-        out_shape=jax.ShapeDtypeStruct((1, items), jnp.float32),
-        in_specs=[VMEM],
-        out_specs=VMEM,
+        functools.partial(prepare_kernel, n, owners),
+        out_shape=(
+            jax.ShapeDtypeStruct((1, items), jnp.float32),
+            jax.ShapeDtypeStruct((2, rows, LANES), jnp.float32),
+        ),
+        in_specs=[VMEM] * 3,
+        out_specs=(VMEM, VMEM),
         scratch_shapes=[
             pltpu.VMEM((n, 1, items), jnp.float32),
+            pltpu.VMEM((owners, 2, rows, LANES), jnp.float32),
+            pltpu.VMEM((owners, 2, rows, LANES), jnp.float32),
             pltpu.SemaphoreType.DMA((n,)),
             pltpu.SemaphoreType.DMA((n,)),
+            pltpu.SemaphoreType.DMA((owners,)),
+            pltpu.SemaphoreType.DMA((owners,)),
         ],
-        compiler_params=pltpu.CompilerParams(collective_id=0, has_side_effects=True, vmem_limit_bytes=VMEM_BYTES),
-        cost_estimate=pl.CostEstimate(flops=0, bytes_accessed=16 * 2**20, transcendentals=0),
-        name="scales",
-    )(embeddings)
+        compiler_params=pltpu.CompilerParams(collective_id=0, has_side_effects=True, vmem_limit_bytes=16 * MIB),
+        cost_estimate=pl.CostEstimate(flops=0, bytes_accessed=16 * MIB, transcendentals=0),
+        name="prepare",
+    )(embeddings, first_codes[None, :], second_codes[None, :])
 
 
 def clear(piles):
     rows = piles[0].shape[0]
-    step = min(rows, 256)
+    step = min(rows, 64)
 
     @pl.loop(0, rows // step)
     def _(at):
@@ -95,12 +144,15 @@
 
 def merge(piles):
     rows = piles[0].shape[0]
-    step = min(rows, 256)
+    step = min(rows, 64)
 
     @pl.loop(0, rows // step)
     def _(at):
         where = pl.ds(pl.multiple_of(at * step, step), step)
-        piles[0][where, :] = (piles[0][where, :] + piles[1][where, :]) + (piles[2][where, :] + piles[3][where, :])
+        parts = [pile[where, :] for pile in piles]
+        while len(parts) > 1:
+            parts = [a + b for a, b in zip(parts[::2], parts[1::2])]
+        piles[0][where, :] = parts[0]
 
 
 def add_rows(piles, codes, rows):
@@ -115,21 +167,23 @@
         piles[at][pl.ds(codes[at + PILES], 1), :] = second[at]
 
 
-def first_kernel(codes_ref, e_ref, scale_ref, normed_ref, sums_ref, *more):
+def first_kernel(codes_ref, e_ref, scale_ref, normed_ref, sums_ref, left, right, *more):
     piles = (sums_ref,) + more
     items = e_ref.shape[1]
     clear(piles)
 
-    @pl.loop(0, items // LANES)
-    def _(at):
-        span = pl.ds(pl.multiple_of(at * LANES, LANES), LANES)
-        normed_ref[span, :] = (e_ref[:, span].astype(jnp.float32) * scale_ref[:, span]).T
-
-    @pl.loop(0, items // GROUP, unroll=2)
-    def _(at):
-        base = pl.multiple_of(at * GROUP, GROUP)
-        rows = [normed_ref[pl.ds(base + j, 1), :] for j in range(GROUP)]
-        add_rows(piles, [codes_ref[base + j] for j in range(GROUP)], rows)
+    @pl.loop(0, items // (2 * LANES))
+    def _(at):
+        base = pl.multiple_of(at * 2 * LANES, 2 * LANES)
+        for which, stage in enumerate((left, right)):
+            span = pl.ds(pl.multiple_of(base + which * LANES, LANES), LANES)
+            block = (e_ref[:, span].astype(jnp.float32) * scale_ref[:, span]).T
+            stage[...] = block
+            normed_ref[span, :] = block
+        for which, stage in enumerate((left, right)):
+            for start in range(0, LANES, GROUP):
+                rows = [stage[start + j:start + j + 1, :] for j in range(GROUP)]
+                add_rows(piles, [codes_ref[base + which * LANES + start + j] for j in range(GROUP)], rows)
 
     merge(piles)
 
@@ -139,36 +193,39 @@
     items = normed_ref.shape[0]
     clear(piles)
 
-    @pl.loop(0, items // GROUP, unroll=2)
-    def _(at):
-        base = pl.multiple_of(at * GROUP, GROUP)
-        rows = [
-            normed_ref[pl.ds(base + j, 1), :] - table_ref[pl.ds(first_ref[base + j], 1), :] for j in range(GROUP)
-        ]
-        add_rows(piles, [second_ref[base + j] for j in range(GROUP)], rows)
-        for j in range(GROUP):
-            middle_ref[pl.ds(base + j, 1), :] = rows[j]
+    @pl.loop(0, items // SPAN)
+    def _(at):
+        for start in range(0, SPAN, GROUP):
+            base = pl.multiple_of(at * SPAN + start, GROUP)
+            rows = [
+                normed_ref[pl.ds(base + j, 1), :] - table_ref[pl.ds(first_ref[base + j], 1), :] for j in range(GROUP)
+            ]
+            add_rows(piles, [second_ref[base + j] for j in range(GROUP)], rows)
+            for j in range(GROUP):
+                middle_ref[pl.ds(base + j, 1), :] = rows[j]
 
     merge(piles)
 
 
-def last_kernel(block, codes_ref, middle_ref, table_ref, out_ref, named):
+def last_kernel(block, codes_ref, middle_ref, table_ref, out_ref, left, right):
     start = pl.program_id(0) * block
 
-    @pl.loop(0, block // GROUP, unroll=2)
-    def _(at):
-        base = pl.multiple_of(at * GROUP, GROUP)
-        rows = [table_ref[pl.ds(codes_ref[start + base + j], 1), :] for j in range(GROUP)]
-        for j in range(GROUP):
-            named[pl.ds(base + j, 1), :] = rows[j]
-
-    @pl.loop(0, block // LANES)
-    def _(at):
-        span = pl.ds(pl.multiple_of(at * LANES, LANES), LANES)
-        out_ref[:, span] = (middle_ref[span, :] - named[span, :]).T
-
-
-def exchange_kernel(n, sums_ref, old_ref, inverse_ref, whole_ref, own_ref, slots, send_in, recv_in, send_out, recv_out):
+    @pl.loop(0, block // (2 * LANES))
+    def _(at):
+        base = pl.multiple_of(at * 2 * LANES, 2 * LANES)
+        for which, stage in enumerate((left, right)):
+            for group in range(0, LANES, GROUP):
+                rows = [
+                    table_ref[pl.ds(codes_ref[start + base + which * LANES + group + j], 1), :] for j in range(GROUP)
+                ]
+                for j in range(GROUP):
+                    stage[group + j:group + j + 1, :] = rows[j]
+        for which, stage in enumerate((left, right)):
+            span = pl.ds(pl.multiple_of(base + which * LANES, LANES), LANES)
+            out_ref[:, span] = (middle_ref[span, :] - stage[...]).T
+
+
+def exchange_kernel(n, sums_ref, old_ref, inverse_ref, whole_ref, own_ref, old, inverse, slots, send_in, recv_in, send_out, recv_out):
     levels = n.bit_length() - 1
     me = lax.axis_index("item")
     size = sums_ref.shape[0] // n
@@ -226,6 +283,10 @@
     for fars in zip(*(subsets(order[1:], (1, 0)) for order in orders)):
         for path, far in enumerate(fars):
             send_sum(path, 0, far, sums_ref.at[block(flip(me, (0,) + far), path)])
+    for at in range(size // LANES):
+        span = slice(at * LANES, (at + 1) * LANES)
+        old[span, :] = (0.5 * old_ref[:, span]).T
+        inverse[span, :] = jnp.broadcast_to(inverse_ref[at:at + 1, :], (old.shape[1], LANES)).T
     for step in range(levels):
         for fars in zip(*(subsets(order[step + 1:], (1, 0)) for order in orders)):
             for path, far in enumerate(fars):
@@ -250,11 +311,14 @@
                         send_sum(path, step + 1, tuple(b for b in far if b != ahead), slots.at[slot])
                 else:
                     rows = pl.ds(path * half, half)
-                    new = old_ref[rows, :] + total * inverse_ref[rows, :]
-                    own_ref[rows, :] = new
+                    new = old[rows, :] + total * inverse[rows, :]
                     whole_ref[block(me, path), :] = new
                     for later in range(levels):
                         send_new(path, later, ())
+                    for at in range(half // LANES):
+                        own_ref[:, path * half + at * LANES:path * half + (at + 1) * LANES] = new[
+                            at * LANES:(at + 1) * LANES, :
+                        ].T
 
     for step in range(levels):
         for helds in zip(*(subsets(order[::-1][:step], (0, 1)) for order in orders)):
@@ -273,10 +337,12 @@
     count = 2 * (n - 1)
     return pl.pallas_call(
         functools.partial(exchange_kernel, n),
-        out_shape=(jax.ShapeDtypeStruct(sums.shape, jnp.float32), jax.ShapeDtypeStruct((size, width), jnp.float32)),
+        out_shape=(jax.ShapeDtypeStruct(sums.shape, jnp.float32), jax.ShapeDtypeStruct((width, size), jnp.float32)),
         in_specs=[VMEM] * 3,
         out_specs=(VMEM, VMEM),
         scratch_shapes=[
+            pltpu.VMEM((size, width), jnp.float32),
+            pltpu.VMEM((size, width), jnp.float32),
             pltpu.VMEM((count, size // 2, width), jnp.float32),
             pltpu.SemaphoreType.DMA((count,)),
             pltpu.SemaphoreType.DMA((count,)),
@@ -284,64 +350,46 @@
             pltpu.SemaphoreType.DMA((count,)),
         ],
         compiler_params=pltpu.CompilerParams(
-            collective_id=collective_id, has_side_effects=True, vmem_limit_bytes=VMEM_BYTES
+            collective_id=collective_id, has_side_effects=True, vmem_limit_bytes=18 * MIB
         ),
         cost_estimate=pl.CostEstimate(flops=0, bytes_accessed=128 * 2**20, transcendentals=0),
         name="exchange",
     )(sums, old, inverse)
 
 
-def counts_of(codes, total):
-    high = lax.shift_right_logical(codes, 7)[None, :] == jnp.arange(total // LANES, dtype=codes.dtype)[:, None]
-    low = lax.bitwise_and(codes, LANES - 1)[None, :] == jnp.arange(LANES, dtype=codes.dtype)[:, None]
-    return lax.dot_general(
-        high.astype(jnp.bfloat16),
-        low.astype(jnp.bfloat16),
-        (((1,), (1,)), ((), ())),
-        preferred_element_type=jnp.float32,
-    )
-
-
 def on_device(owners, feature_parts, embeddings, first_codes, second_codes, first_old, second_old):
     width, items = embeddings.shape
     total = first_old.shape[1] * owners
     f32 = jnp.float32
-    local = pltpu.CompilerParams(vmem_limit_bytes=VMEM_BYTES)
-    cost = pl.CostEstimate(flops=0, bytes_accessed=64 * 2**20, transcendentals=0)
-
-    counts = jnp.stack([counts_of(first_codes, total), counts_of(second_codes, total)], axis=1)
-    counts = lax.psum_scatter(counts, "item", scatter_dimension=0, tiled=True)
-    halves = 0.5 / (counts + 1.0)
-    first_inverse, second_inverse = (
-        jnp.broadcast_to(halves[:, level].reshape(-1, 1), (total // owners, width)) for level in range(2)
-    )
+    cost = pl.CostEstimate(flops=0, bytes_accessed=64 * MIB, transcendentals=0)
     piles = [pltpu.VMEM((total, width), f32)] * (PILES - 1)
     row_sums = jax.ShapeDtypeStruct((total, width), f32)
     row_items = jax.ShapeDtypeStruct((items, width), f32)
 
-    scales = scales_of(embeddings, feature_parts)
+    stage = pltpu.VMEM((LANES, width), f32)
+    scales, inverse = prepare(embeddings, first_codes, second_codes, feature_parts, owners, total)
     normed, first_sums = pl.pallas_call(
         first_kernel,
         out_shape=(row_items, row_sums),
         in_specs=[SMEM, VMEM, VMEM],
         out_specs=(VMEM, VMEM),
-        scratch_shapes=piles,
-        compiler_params=local,
+        scratch_shapes=[stage, stage] + piles,
+        compiler_params=pltpu.CompilerParams(vmem_limit_bytes=44 * MIB),
         cost_estimate=cost,
         name="first_sums",
     )(first_codes, embeddings, scales)
-    first_whole, first_own = exchange(first_sums, 0.5 * first_old.T, first_inverse, owners, 1)
+    first_whole, first_own = exchange(first_sums, first_old, inverse[0], owners, 1)
     middle, second_sums = pl.pallas_call(
         second_kernel,
         out_shape=(row_items, row_sums),
         in_specs=[SMEM, SMEM, VMEM, VMEM],
         out_specs=(VMEM, VMEM),
         scratch_shapes=piles,
-        compiler_params=local,
+        compiler_params=pltpu.CompilerParams(vmem_limit_bytes=48 * MIB),
         cost_estimate=cost,
         name="second_sums",
     )(first_codes, second_codes, normed, first_whole)
-    second_whole, second_own = exchange(second_sums, 0.5 * second_old.T, second_inverse, owners, 2)
+    second_whole, second_own = exchange(second_sums, second_old, inverse[1], owners, 2)
     block = min(items, 1024)
     leftover = pl.pallas_call(
         functools.partial(last_kernel, block),
@@ -353,12 +401,12 @@
             pl.BlockSpec((total, width), lambda at: (0, 0)),
         ],
         out_specs=pl.BlockSpec((width, block), lambda at: (0, at)),
-        scratch_shapes=[pltpu.VMEM((block, width), f32)],
-        compiler_params=local,
+        scratch_shapes=[stage, stage],
+        compiler_params=pltpu.CompilerParams(vmem_limit_bytes=20 * MIB),
         cost_estimate=cost,
         name="leftover",
     )(second_codes, middle, second_whole)
-    return (first_own.T, second_own.T, leftover)
+    return (first_own, second_own, leftover)
 
 
 def solution(mesh):

time: 200 us -> 175 us (0.88)
  Pallas kernels: 178 us -> 159 us
  between operations: 14.2 us -> 0.71 us
  local copies, waits for them, and re-layouts: 2.78 us -> 14.9 us
  other arithmetic: 3.02 us -> 0 us
  matrix products: 2.04 us -> 0 us
    unnamed x12 -> x28, local copies, waits for them, and re-layouts: 2.39 us -> 14.9 us
    pallas_call x2, Pallas kernels: 97 us -> 86.9 us  [exchange(): pl.pallas_call(functools.partial(exchange_kernel, n), out_shape=(jax.Shap...]
    pallas_call x1, Pallas kernels: 26.8 us -> 19.9 us  [on_device(): pl.pallas_call(first_kernel, out_shape=(row_items, row_sums), in_specs=[S...]
    pallas_call x1, Pallas kernels: 18.8 us -> 12.6 us  [on_device(): pl.pallas_call(functools.partial(last_kernel, block), out_shape=jax.Shape...]
    pallas_call x1, Pallas kernels: 8.4 us -> 12.5 us  [prepare(): pl.pallas_call(functools.partial(prepare_kernel, n, owners), out_shape=(j...]
    dot_general x2 -> x0, matrix products: 2.04 us -> none  [counts_of(): lax.dot_general(high.astype(jnp.bfloat16), low.astype(jnp.bfloat16), (((1...]
  transfers between devices with their start and end apart: 1 -> 0, of which waited for: 0 -> 0; matrix products, arithmetic and copies ran while one was open for 0% -> 0% of each run, Pallas kernels for 18% -> 0%
where the time goes in v2:
time: 175 us
  Pallas kernels  159 us (91%)
  local copies, waits for them, and re-layouts  14.9 us (9%)
    pallas_call x2, Pallas kernels, exchange(): pl.pallas_call(functools.partial(exchange_kernel, n), out_shape=(jax.Shap...  86.9 us
    pallas_call x1, Pallas kernels, on_device(): pl.pallas_call(second_kernel, out_shape=(row_items, row_sums), in_specs=[...  27.3 us
    pallas_call x1, Pallas kernels, on_device(): pl.pallas_call(first_kernel, out_shape=(row_items, row_sums), in_specs=[S...  19.9 us
    unnamed x28, local copies, waits for them, and re-layouts  14.9 us
    pallas_call x1, Pallas kernels, on_device(): pl.pallas_call(functools.partial(last_kernel, block), out_shape=jax.Shape...  12.6 us
    pallas_call x1, Pallas kernels, prepare(): pl.pallas_call(functools.partial(prepare_kernel, n, owners), out_shape=(j...  12.5 us

profile of v2, /device:TPU:1, one launch (start us, length us, event | category | flops | bytes accessed | tf_op | source)
XLA Modules:
  0.0 174.9 jit_solution(2795553327414020503)
XLA Ops:
  0.6 0.0 copy-start
  0.6 1.6 copy-done
  2.2 0.0 copy-start.8
  2.2 0.8 copy-done.8
  3.0 0.0 copy-start.11
  3.0 0.8 copy-done.11
  3.7 0.0 copy-start.6
  3.7 0.0 copy-start.10
  3.7 0.0 copy-start.12
  3.7 12.5 %prepare.1 = (f32[1,8192]{1,0:T(1,128)S(1)}, f32[2,8,128]{2,1,0:T(8,128)S(1)}) custom-call(bf16[128,8192]{1,0:T(8,128)(2,1)S(1)} %copy-done, s32[1,8192]{1,0:T(1,128)S(1)} %bitcast.6, s32[1,8192]{1,0:T(1,128)S(1)} %bitcast.7), custom_call_target="tpu_custom_call" | custom-call | bytes 16777216 | tf_op jit(solution)/shard_map/prepare/pallas_call | solution.py:112
  16.2 0.0 copy-start.1
  16.3 1.6 copy-done.1
  17.8 0.0 copy-start.9
  17.8 0.8 copy-done.9
  18.6 19.9 %first_sums.1 = (f32[8192,128]{1,0:T(8,128)S(1)}, f32[8192,128]{1,0:T(8,128)}) custom-call(s32[8192]{0:T(1024)S(1)} %copy-done.9, bf16[128,8192]{1,0:T(8,128)(2,1)S(1)} %copy-done.1, f32[1,8192]{1,0:T(1,128)S(1)} %get-tuple-element.13.scale_ref), custom_call_target="tpu_custom_call" | custom-call | bytes 67108864 | tf_op jit(solution)/shard_map/first_sums/pallas_call | solution.py:371
  38.5 0.0 copy-start.2
  38.5 0.0 copy-done.6
  38.5 0.0 copy-start.5
  38.5 3.7 %copy-done.5 = f32[8192,128]{1,0:T(8,128)S(1)} copy-done((f32[8192,128]{1,0:T(8,128)S(1)}, f32[8192,128]{1,0:T(8,128)}, u32[]{:S(2)}) %copy-start.5) | copy-done | bytes 4194328
  42.3 43.9 %exchange.2 = (f32[8192,128]{1,0:T(8,128)S(1)}, f32[128,1024]{1,0:T(8,128)S(1)}) custom-call(f32[8192,128]{1,0:T(8,128)S(1)} %copy-done.5, f32[128,1024]{1,0:T(8,128)S(1)} %copy-done.6, f32[8,128]{1,0:T(8,128)S(1)} %get-tuple-element.24.inverse_ref), custom_call_target="tpu_custom_call" | custom-call | bytes 134217728 | tf_op jit(solution)/shard_map/exchange/pallas_call | solution.py:338
  86.2 0.0 copy-start.3
  86.2 2.0 %copy-done.3 = f32[8192,128]{1,0:T(8,128)} copy-done((f32[8192,128]{1,0:T(8,128)}, f32[8192,128]{1,0:T(8,128)S(1)}, u32[]{:S(2)}) %copy-start.3) | copy-done | bytes 4194328
  88.2 0.0 copy-done.2
  88.2 0.0 copy-done.10
  88.2 0.0 copy-done.12
  88.2 0.0 copy-start.7
  88.2 27.3 %second_sums.1 = (f32[8192,128]{1,0:T(8,128)S(1)}, f32[8192,128]{1,0:T(8,128)}) custom-call(s32[8192]{0:T(1024)S(1)} %copy-done.10, s32[8192]{0:T(1024)S(1)} %copy-done.12, f32[8192,128]{1,0:T(8,128)} %copy-done.2, f32[8192,128]{1,0:T(8,128)} %copy-done.3), custom_call_target="tpu_custom_call" | custom-call | bytes 67108864 | tf_op jit(solution)/shard_map/second_sums/pallas_call | solution.py:382
  115.6 0.0 copy-done.7
  115.6 0.0 copy-start.4
  115.6 2.2 %copy-done.4 = f32[8192,128]{1,0:T(8,128)S(1)} copy-done((f32[8192,128]{1,0:T(8,128)S(1)}, f32[8192,128]{1,0:T(8,128)}, u32[]{:S(2)}) %copy-start.4) | copy-done | bytes 4194328
  117.8 43.0 %exchange.3 = (f32[8192,128]{1,0:T(8,128)S(1)}, f32[128,1024]{1,0:T(8,128)S(1)}) custom-call(f32[8192,128]{1,0:T(8,128)S(1)} %copy-done.4, f32[128,1024]{1,0:T(8,128)S(1)} %copy-done.7, f32[8,128]{1,0:T(8,128)S(1)} %get-tuple-element.23.inverse_ref), custom_call_target="tpu_custom_call" | custom-call | bytes 134217728 | tf_op jit(solution)/shard_map/exchange/pallas_call | solution.py:338
  160.7 12.6 %leftover.1 = f32[128,8192]{1,0:T(8,128)} custom-call(s32[8192]{0:T(1024)S(1)} %copy-done.12, f32[8192,128]{1,0:T(8,128)S(1)} %get-tuple-element.21.middle_ref, f32[8192,128]{1,0:T(8,128)S(1)} %get-tuple-element.22.table_ref), custom_call_target="tpu_custom_call" | custom-call | bytes 67108864 | tf_op jit(solution)/shard_map/leftover/pallas_call | solution.py:394
  173.4 0.8 copy.10
  174.1 0.8 copy.11
  (1 shorter events, 0.0 us)
Async XLA Ops:
  0.6 1.6 copy-start
  2.2 0.8 copy-start.8
  3.0 0.8 copy-start.11
  3.7 34.8 %copy-start.6 = (f32[128,1024]{1,0:T(8,128)S(1)}, f32[128,1024]{1,0:T(8,128)}, u32[]{:S(2)}) copy-start(f32[128,1024]{1,0:T(8,128)} %old_ref.2) | copy-start | bytes 1572868
  3.7 84.5 %copy-start.10 = (s32[8192]{0:T(1024)S(1)}, s32[8192]{0:T(1024)}, u32[]{:S(2)}) copy-start(s32[8192]{0:T(1024)} %first_ref.1) | copy-start | bytes 98308
  3.7 84.5 %copy-start.12 = (s32[8192]{0:T(1024)S(1)}, s32[8192]{0:T(1024)}, u32[]{:S(2)}) copy-start(s32[8192]{0:T(1024)} %codes_ref.3) | copy-start | bytes 98308
  16.2 1.6 copy-start.1
  17.8 0.8 copy-start.9
  38.5 49.7 %copy-start.2 = (f32[8192,128]{1,0:T(8,128)}, f32[8192,128]{1,0:T(8,128)S(1)}, u32[]{:S(2)}) copy-start(f32[8192,128]{1,0:T(8,128)S(1)} %get-tuple-element.17.normed_ref) | copy-start | bytes 12582916
  38.5 3.7 %copy-start.5 = (f32[8192,128]{1,0:T(8,128)S(1)}, f32[8192,128]{1,0:T(8,128)}, u32[]{:S(2)}) copy-start(f32[8192,128]{1,0:T(8,128)} %get-tuple-element.14.sums_ref) | copy-start | bytes 12582916
  86.2 2.0 %copy-start.3 = (f32[8192,128]{1,0:T(8,128)}, f32[8192,128]{1,0:T(8,128)S(1)}, u32[]{:S(2)}) copy-start(f32[8192,128]{1,0:T(8,128)S(1)} %get-tuple-element.18.table_ref) | copy-start | bytes 12582916
  88.2 27.3 %copy-start.7 = (f32[128,1024]{1,0:T(8,128)S(1)}, f32[128,1024]{1,0:T(8,128)}, u32[]{:S(2)}) copy-start(f32[128,1024]{1,0:T(8,128)} %old_ref.3) | copy-start | bytes 1572868
  115.6 2.2 %copy-start.4 = (f32[8192,128]{1,0:T(8,128)S(1)}, f32[8192,128]{1,0:T(8,128)}, u32[]{:S(2)}) copy-start(f32[8192,128]{1,0:T(8,128)} %get-tuple-element.19.sums_ref) | copy-start | bytes 12582916

commit v3 on v2

--- a/solution.py
+++ b/solution.py
@@ -12,11 +12,15 @@
 LANES = 128
 PILES = 8
 GROUP = 2 * PILES
-SPAN = 64
+SPAN = 128
+BLOCK = 1024
+PATHS = 4
 MIB = 2**20
+VMEM_BYTES = 56 * MIB
 
 VMEM = pl.BlockSpec(memory_space=pltpu.VMEM)
 SMEM = pl.BlockSpec(memory_space=pltpu.SMEM)
+ANY = pl.BlockSpec(memory_space=pl.ANY)
 
 
 def flip(me, bits):
@@ -126,7 +130,7 @@
             pltpu.SemaphoreType.DMA((owners,)),
             pltpu.SemaphoreType.DMA((owners,)),
         ],
-        compiler_params=pltpu.CompilerParams(collective_id=0, has_side_effects=True, vmem_limit_bytes=16 * MIB),
+        compiler_params=pltpu.CompilerParams(collective_id=0, has_side_effects=True, vmem_limit_bytes=VMEM_BYTES),
         cost_estimate=pl.CostEstimate(flops=0, bytes_accessed=16 * MIB, transcendentals=0),
         name="prepare",
     )(embeddings, first_codes[None, :], second_codes[None, :])
@@ -170,7 +174,11 @@
 def first_kernel(codes_ref, e_ref, scale_ref, normed_ref, sums_ref, left, right, *more):
     piles = (sums_ref,) + more
     items = e_ref.shape[1]
-    clear(piles)
+    offset = pl.program_id(0) * items
+
+    @pl.when(pl.program_id(0) == 0)
+    def _():
+        clear(piles)
 
     @pl.loop(0, items // (2 * LANES))
     def _(at):
@@ -183,32 +191,47 @@
         for which, stage in enumerate((left, right)):
             for start in range(0, LANES, GROUP):
                 rows = [stage[start + j:start + j + 1, :] for j in range(GROUP)]
-                add_rows(piles, [codes_ref[base + which * LANES + start + j] for j in range(GROUP)], rows)
-
-    merge(piles)
-
-
-def second_kernel(first_ref, second_ref, normed_ref, table_ref, middle_ref, sums_ref, *more):
+                add_rows(piles, [codes_ref[offset + base + which * LANES + start + j] for j in range(GROUP)], rows)
+
+    @pl.when(pl.program_id(0) == pl.num_programs(0) - 1)
+    def _():
+        merge(piles)
+
+
+def second_kernel(first_ref, second_ref, normed_ref, table_ref, own_ref, middle_ref, sums_ref, new_ref, *more):
     piles = (sums_ref,) + more
     items = normed_ref.shape[0]
-    clear(piles)
+    offset = pl.program_id(0) * items
+
+    @pl.when(pl.program_id(0) == 0)
+    def _():
+        new_ref[...] = own_ref[...]
+        clear(piles)
 
     @pl.loop(0, items // SPAN)
     def _(at):
         for start in range(0, SPAN, GROUP):
             base = pl.multiple_of(at * SPAN + start, GROUP)
             rows = [
-                normed_ref[pl.ds(base + j, 1), :] - table_ref[pl.ds(first_ref[base + j], 1), :] for j in range(GROUP)
+                normed_ref[pl.ds(base + j, 1), :] - table_ref[pl.ds(first_ref[offset + base + j], 1), :]
+                for j in range(GROUP)
             ]
-            add_rows(piles, [second_ref[base + j] for j in range(GROUP)], rows)
+            add_rows(piles, [second_ref[offset + base + j] for j in range(GROUP)], rows)
             for j in range(GROUP):
                 middle_ref[pl.ds(base + j, 1), :] = rows[j]
 
-    merge(piles)
-
-
-def last_kernel(block, codes_ref, middle_ref, table_ref, out_ref, left, right):
+    @pl.when(pl.program_id(0) == pl.num_programs(0) - 1)
+    def _():
+        merge(piles)
+
+
+def last_kernel(codes_ref, middle_ref, table_ref, own_ref, out_ref, new_ref, left, right):
+    block = middle_ref.shape[0]
     start = pl.program_id(0) * block
+
+    @pl.when(pl.program_id(0) == 0)
+    def _():
+        new_ref[...] = own_ref[...]
 
     @pl.loop(0, block // (2 * LANES))
     def _(at):
@@ -225,16 +248,19 @@
             out_ref[:, span] = (middle_ref[span, :] - stage[...]).T
 
 
-def exchange_kernel(n, sums_ref, old_ref, inverse_ref, whole_ref, own_ref, old, inverse, slots, send_in, recv_in, send_out, recv_out):
+def exchange_kernel(
+    n, sums_ref, old_ref, inverse_ref, whole_ref, own_ref, old, inverse, fresh, kept, slots,
+    keep_sems, own_sems, send_in, recv_in, send_out, recv_out
+):
     levels = n.bit_length() - 1
     me = lax.axis_index("item")
     size = sums_ref.shape[0] // n
-    half = size // 2
+    part = size // PATHS
     rest = list(range(1, levels))
-    orders = ([0] + rest, [0] + rest[::-1])
+    orders = [[0] + (rest if path % 2 == 0 else rest[::-1]) for path in range(PATHS)]
 
     def block(owner, path):
-        return pl.ds(pl.multiple_of(owner * size + path * half, half), half)
+        return pl.ds(pl.multiple_of(owner * size + path * part, part), part)
 
     place_in, place_out = {}, {}
     for path, order in enumerate(orders):
@@ -243,12 +269,17 @@
                 place_in[path, step, frozenset(far)] = len(place_in)
             for held in subsets(order[::-1][:step], (0, 1)):
                 place_out[path, step, frozenset(held)] = len(place_out)
-
+    place_kept = {
+        (path, frozenset(far)): at
+        for at, (path, far) in enumerate(
+            (path, far) for path in range(PATHS) for far in subsets(orders[path][1:], (1, 0))
+        )
+    }
     sent = []
 
-    def send_sum(path, step, far, source):
+    def sum_copy(path, step, far, source):
         slot = place_in[path, step, frozenset(far)]
-        copy = pltpu.make_async_remote_copy(
+        return pltpu.make_async_remote_copy(
             src_ref=source,
             dst_ref=slots.at[slot],
             send_sem=send_in.at[slot],
@@ -256,13 +287,11 @@
             device_id={"item": flip(me, [orders[path][step]])},
             device_id_type=pl.DeviceIdType.MESH,
         )
-        copy.start()
-        sent.append(copy)
-
-    def new_copy(path, step, held, rows):
+
+    def new_copy(path, step, held, source, rows):
         slot = place_out[path, step, frozenset(held)]
         return pltpu.make_async_remote_copy(
-            src_ref=whole_ref.at[rows],
+            src_ref=source,
             dst_ref=whole_ref.at[rows],
             send_sem=send_out.at[slot],
             recv_sem=recv_out.at[slot],
@@ -270,37 +299,44 @@
             device_id_type=pl.DeviceIdType.MESH,
         )
 
-    def send_new(path, step, held):
-        copy = new_copy(path, step, held, block(flip(me, held), path))
+    def send(copy):
         copy.start()
         sent.append(copy)
+
+    def keep_copy(path, far):
+        slot = place_kept[path, frozenset(far)]
+        return pltpu.make_async_copy(sums_ref.at[block(flip(me, far), path)], kept.at[slot], keep_sems.at[slot])
+
+    def fars_of(step):
+        return list(zip(*(subsets(order[step + 1:], (1, 0)) for order in orders)))
+
+    def open_with(fars):
+        for path, far in enumerate(fars):
+            send(sum_copy(path, 0, far, sums_ref.at[block(flip(me, (0,) + far), path)]))
 
     barrier = pltpu.get_barrier_semaphore()
     for bit in range(levels):
         pl.semaphore_signal(barrier, inc=1, device_id={"item": flip(me, [bit])}, device_id_type=pl.DeviceIdType.MESH)
+    for fars in fars_of(0):
+        for path, far in enumerate(fars):
+            keep_copy(path, far).start()
     pl.semaphore_wait(barrier, levels)
 
-    for fars in zip(*(subsets(order[1:], (1, 0)) for order in orders)):
-        for path, far in enumerate(fars):
-            send_sum(path, 0, far, sums_ref.at[block(flip(me, (0,) + far), path)])
-    for at in range(size // LANES):
-        span = slice(at * LANES, (at + 1) * LANES)
-        old[span, :] = (0.5 * old_ref[:, span]).T
-        inverse[span, :] = jnp.broadcast_to(inverse_ref[at:at + 1, :], (old.shape[1], LANES)).T
+    opening = fars_of(0)
+    middle = len(opening) // 2
+    for fars in opening[:middle]:
+        open_with(fars)
     for step in range(levels):
-        for fars in zip(*(subsets(order[step + 1:], (1, 0)) for order in orders)):
+        for at, fars in enumerate(fars_of(step)):
+            if step == 0 and at == middle:
+                for later in opening[middle:]:
+                    open_with(later)
             for path, far in enumerate(fars):
                 slot = place_in[path, step, frozenset(far)]
-                pltpu.make_async_remote_copy(
-                    src_ref=slots.at[slot],
-                    dst_ref=slots.at[slot],
-                    send_sem=send_in.at[slot],
-                    recv_sem=recv_in.at[slot],
-                    device_id={"item": flip(me, [orders[path][step]])},
-                    device_id_type=pl.DeviceIdType.MESH,
-                ).wait_recv()
+                sum_copy(path, step, far, slots.at[slot]).wait_recv()
                 if step == 0:
-                    mine = sums_ref[block(flip(me, far), path), :]
+                    keep_copy(path, far).wait()
+                    mine = kept[place_kept[path, frozenset(far)]]
                 else:
                     mine = slots[place_in[path, step - 1, frozenset(far)]]
                 total = slots[slot] + mine
@@ -308,25 +344,35 @@
                     slots[slot] = total
                     ahead = orders[path][step + 1]
                     if ahead in far:
-                        send_sum(path, step + 1, tuple(b for b in far if b != ahead), slots.at[slot])
+                        send(sum_copy(path, step + 1, tuple(b for b in far if b != ahead), slots.at[slot]))
                 else:
-                    rows = pl.ds(path * half, half)
-                    new = old[rows, :] + total * inverse[rows, :]
-                    whole_ref[block(me, path), :] = new
+                    rows = pl.ds(path * part, part)
+                    fresh[rows, :] = old[rows, :] + total * inverse[rows, :]
                     for later in range(levels):
-                        send_new(path, later, ())
-                    for at in range(half // LANES):
-                        own_ref[:, path * half + at * LANES:path * half + (at + 1) * LANES] = new[
-                            at * LANES:(at + 1) * LANES, :
-                        ].T
+                        send(new_copy(path, later, (), fresh.at[rows], block(me, path)))
+                    pltpu.make_async_copy(fresh.at[rows], whole_ref.at[block(me, path)], own_sems.at[path]).start()
+        if step == 0:
+            for at in range(size // LANES):
+                span = slice(at * LANES, (at + 1) * LANES)
+                old[span, :] = (0.5 * old_ref[:, span]).T
+                inverse[span, :] = jnp.broadcast_to(inverse_ref[at:at + 1, :], (old.shape[1], LANES)).T
 
     for step in range(levels):
         for helds in zip(*(subsets(order[::-1][:step], (0, 1)) for order in orders)):
             for path, held in enumerate(helds):
                 got = held + (orders[path][::-1][step],)
-                new_copy(path, step, held, block(flip(me, got), path)).wait_recv()
+                rows = block(flip(me, got), path)
+                new_copy(path, step, held, whole_ref.at[rows], rows).wait_recv()
                 for later in range(step + 1, levels):
-                    send_new(path, later, got)
+                    send(new_copy(path, later, got, whole_ref.at[rows], rows))
+        if step == 0:
+            for at in range(size // LANES):
+                span = slice(at * LANES, (at + 1) * LANES)
+                own_ref[:, span] = fresh[span, :].T
+    for path in range(PATHS):
+        pltpu.make_async_copy(
+            fresh.at[pl.ds(path * part, part)], whole_ref.at[block(me, path)], own_sems.at[path]
+        ).wait()
     for copy in sent:
         copy.wait_send()
 
@@ -334,25 +380,30 @@
 def exchange(sums, old, inverse, n, collective_id):
     rows, width = sums.shape
     size = rows // n
-    count = 2 * (n - 1)
+    part = size // PATHS
+    count = PATHS * (n - 1)
     return pl.pallas_call(
         functools.partial(exchange_kernel, n),
         out_shape=(jax.ShapeDtypeStruct(sums.shape, jnp.float32), jax.ShapeDtypeStruct((width, size), jnp.float32)),
-        in_specs=[VMEM] * 3,
-        out_specs=(VMEM, VMEM),
+        in_specs=[ANY, VMEM, VMEM],
+        out_specs=(ANY, VMEM),
         scratch_shapes=[
             pltpu.VMEM((size, width), jnp.float32),
             pltpu.VMEM((size, width), jnp.float32),
-            pltpu.VMEM((count, size // 2, width), jnp.float32),
+            pltpu.VMEM((size, width), jnp.float32),
+            pltpu.VMEM((PATHS * n // 2, part, width), jnp.float32),
+            pltpu.VMEM((count, part, width), jnp.float32),
+            pltpu.SemaphoreType.DMA((PATHS * n // 2,)),
+            pltpu.SemaphoreType.DMA((PATHS,)),
             pltpu.SemaphoreType.DMA((count,)),
             pltpu.SemaphoreType.DMA((count,)),
             pltpu.SemaphoreType.DMA((count,)),
             pltpu.SemaphoreType.DMA((count,)),
         ],
         compiler_params=pltpu.CompilerParams(
-            collective_id=collective_id, has_side_effects=True, vmem_limit_bytes=18 * MIB
+            collective_id=collective_id, has_side_effects=True, vmem_limit_bytes=VMEM_BYTES
         ),
-        cost_estimate=pl.CostEstimate(flops=0, bytes_accessed=128 * 2**20, transcendentals=0),
+        cost_estimate=pl.CostEstimate(flops=0, bytes_accessed=128 * MIB, transcendentals=0),
         name="exchange",
     )(sums, old, inverse)
 
@@ -368,45 +419,50 @@
 
     stage = pltpu.VMEM((LANES, width), f32)
     scales, inverse = prepare(embeddings, first_codes, second_codes, feature_parts, owners, total)
+    block = min(items, BLOCK)
+    steps = (items // block,)
+    local = pltpu.CompilerParams(vmem_limit_bytes=VMEM_BYTES)
+    by_rows = pl.BlockSpec((block, width), lambda at: (at, 0))
+    by_columns = pl.BlockSpec((width, block), lambda at: (0, at))
+    table = pl.BlockSpec((total, width), lambda at: (0, 0))
+    own = pl.BlockSpec(first_old.shape, lambda at: (0, 0))
+    own_shape = jax.ShapeDtypeStruct(first_old.shape, f32)
     normed, first_sums = pl.pallas_call(
         first_kernel,
         out_shape=(row_items, row_sums),
-        in_specs=[SMEM, VMEM, VMEM],
-        out_specs=(VMEM, VMEM),
+        grid=steps,
+        in_specs=[SMEM, by_columns, pl.BlockSpec((1, block), lambda at: (0, at))],
+        out_specs=(by_rows, table),
         scratch_shapes=[stage, stage] + piles,
-        compiler_params=pltpu.CompilerParams(vmem_limit_bytes=44 * MIB),
+        compiler_params=local,
         cost_estimate=cost,
         name="first_sums",
     )(first_codes, embeddings, scales)
     first_whole, first_own = exchange(first_sums, first_old, inverse[0], owners, 1)
-    middle, second_sums = pl.pallas_call(
+    middle, second_sums, first_new = pl.pallas_call(
         second_kernel,
-        out_shape=(row_items, row_sums),
-        in_specs=[SMEM, SMEM, VMEM, VMEM],
-        out_specs=(VMEM, VMEM),
+        out_shape=(row_items, row_sums, own_shape),
+        grid=steps,
+        in_specs=[SMEM, SMEM, by_rows, table, own],
+        out_specs=(by_rows, table, own),
         scratch_shapes=piles,
-        compiler_params=pltpu.CompilerParams(vmem_limit_bytes=48 * MIB),
+        compiler_params=local,
         cost_estimate=cost,
         name="second_sums",
-    )(first_codes, second_codes, normed, first_whole)
+    )(first_codes, second_codes, normed, first_whole, first_own)
     second_whole, second_own = exchange(second_sums, second_old, inverse[1], owners, 2)
-    block = min(items, 1024)
-    leftover = pl.pallas_call(
-        functools.partial(last_kernel, block),
-        out_shape=jax.ShapeDtypeStruct((width, items), f32),
-        grid=(items // block,),
-        in_specs=[
-            SMEM,
-            pl.BlockSpec((block, width), lambda at: (at, 0)),
-            pl.BlockSpec((total, width), lambda at: (0, 0)),
-        ],
-        out_specs=pl.BlockSpec((width, block), lambda at: (0, at)),
+    leftover, second_new = pl.pallas_call(
+        last_kernel,
+        out_shape=(jax.ShapeDtypeStruct((width, items), f32), own_shape),
+        grid=steps,
+        in_specs=[SMEM, by_rows, table, own],
+        out_specs=(by_columns, own),
         scratch_shapes=[stage, stage],
-        compiler_params=pltpu.CompilerParams(vmem_limit_bytes=20 * MIB),
+        compiler_params=local,
         cost_estimate=cost,
         name="leftover",
-    )(second_codes, middle, second_whole)
-    return (first_own, second_own, leftover)
+    )(second_codes, middle, second_whole, second_own)
+    return (first_new, second_new, leftover)
 
 
 def solution(mesh):

time: 175 us -> 164 us (0.937)
  local copies, waits for them, and re-layouts: 14.9 us -> 1.29 us
  Pallas kernels: 159 us -> 162 us
    unnamed x28 -> x0, local copies, waits for them, and re-layouts: 14.9 us -> none
    pallas_call x1, Pallas kernels: 12.5 us -> 14.7 us  [prepare(): pl.pallas_call(functools.partial(prepare_kernel, n, owners), out_shape=(j...]
where the time goes in v3:
time: 164 us
  Pallas kernels  162 us (99%)
    pallas_call x2, Pallas kernels, exchange(): pl.pallas_call(functools.partial(exchange_kernel, n), out_shape=(jax.Shap...  86 us
    pallas_call x1, Pallas kernels, on_device(): pl.pallas_call(second_kernel, out_shape=(row_items, row_sums, own_shape),...  26.3 us
    pallas_call x1, Pallas kernels, on_device(): pl.pallas_call(first_kernel, out_shape=(row_items, row_sums), grid=steps,...  20.7 us
    pallas_call x1, Pallas kernels, prepare(): pl.pallas_call(functools.partial(prepare_kernel, n, owners), out_shape=(j...  14.7 us
    pallas_call x1, Pallas kernels, on_device(): pl.pallas_call(last_kernel, out_shape=(jax.ShapeDtypeStruct((width, items...  14.3 us

profile of v3, /device:TPU:1, one launch (start us, length us, event | category | flops | bytes accessed | tf_op | source)
XLA Modules:
  0.0 164.0 jit_solution(16707586925400860095)
XLA Ops:
  0.6 14.7 %prepare.1 = (f32[1,8192]{1,0:T(1,128)}, f32[2,8,128]{2,1,0:T(8,128)}) custom-call(bf16[128,8192]{1,0:T(8,128)(2,1)} %e_ref.3, s32[1,8192]{1,0:T(1,128)} %bitcast.6, s32[1,8192]{1,0:T(1,128)} %bitcast.7), custom_call_target="tpu_custom_call" | custom-call | bytes 16777216 | tf_op jit(solution)/shard_map/prepare/pallas_call | solution.py:116
  15.4 1.3 slice_bitcast_fusion
  16.6 20.7 %first_sums.1 = (f32[8192,128]{1,0:T(8,128)}, f32[8192,128]{1,0:T(8,128)}) custom-call(s32[8192]{0:T(1024)} %first_ref.1, bf16[128,8192]{1,0:T(8,128)(2,1)} %e_ref.3, f32[1,8192]{1,0:T(1,128)} %get-tuple-element.16.scale_ref), custom_call_target="tpu_custom_call" | custom-call | bytes 67108864 | tf_op jit(solution)/shard_map/first_sums/pallas_call | solution.py:430
  37.3 43.2 %exchange.2 = (f32[8192,128]{1,0:T(8,128)}, f32[128,1024]{1,0:T(8,128)}) custom-call(f32[8192,128]{1,0:T(8,128)} %get-tuple-element.18.sums_ref, f32[128,1024]{1,0:T(8,128)} %old_ref.2, f32[8,128]{1,0:T(8,128)} %get-tuple-element.30.inverse_ref), custom_call_target="tpu_custom_call" | custom-call | bytes 134217728 | tf_op jit(solution)/shard_map/exchange/pallas_call | solution.py:385
  80.5 26.3 %second_sums.1 = (f32[8192,128]{1,0:T(8,128)}, f32[8192,128]{1,0:T(8,128)}, f32[128,1024]{1,0:T(8,128)}) custom-call(s32[8192]{0:T(1024)} %first_ref.1, s32[8192]{0:T(1024)} %codes_ref.3, f32[8192,128]{1,0:T(8,128)} %get-tuple-element.17.normed_ref, f32[8192,128]{1,0:T(8,128)} %get-tuple-element.20.table_ref, f32[128,1024]{1,0:T(8,128)} %get-tuple-element.21.own_ref), custom_call_target="tpu_custom_call" | custom-call | bytes 67108864 | tf_op jit(solution)/shard_map/second_sums/pallas_call | solution.py:442
  106.8 42.9 %exchange.3 = (f32[8192,128]{1,0:T(8,128)}, f32[128,1024]{1,0:T(8,128)}) custom-call(f32[8192,128]{1,0:T(8,128)} %get-tuple-element.24.sums_ref, f32[128,1024]{1,0:T(8,128)} %old_ref.3, f32[8,128]{1,0:T(8,128)} %get-tuple-element.29.inverse_ref), custom_call_target="tpu_custom_call" | custom-call | bytes 134217728 | tf_op jit(solution)/shard_map/exchange/pallas_call | solution.py:385
  149.7 14.3 %leftover.1 = (f32[128,8192]{1,0:T(8,128)}, f32[128,1024]{1,0:T(8,128)}) custom-call(s32[8192]{0:T(1024)} %codes_ref.3, f32[8192,128]{1,0:T(8,128)} %get-tuple-element.23.middle_ref, f32[8192,128]{1,0:T(8,128)} %get-tuple-element.25.table_ref, f32[128,1024]{1,0:T(8,128)} %get-tuple-element.26.own_ref), custom_call_target="tpu_custom_call" | custom-call | bytes 67108864 | tf_op jit(solution)/shard_map/leftover/pallas_call | solution.py:454

commit v4 on v3

--- a/solution.py
+++ b/solution.py
@@ -35,18 +35,11 @@
     return [tuple(b for b, c in zip(bits, pick) if c) for pick in itertools.product(choice, repeat=len(bits))]
 
 
-def prepare_kernel(
-    n, owners, e_ref, first_ref, second_ref, scale_ref, inverse_ref, parts, counts, got, send_sems, recv_sems,
-    send_counts, recv_counts
-):
-    me, home = lax.axis_index("code"), lax.axis_index("item")
+def scales_kernel(n, e_ref, scale_ref, parts, send_sems, recv_sems):
+    me = lax.axis_index("code")
     barrier = pltpu.get_barrier_semaphore()
     for step in range(1, n):
         pl.semaphore_signal(barrier, inc=1, device_id={"code": lax.rem(me + step, n)}, device_id_type=pl.DeviceIdType.MESH)
-    for step in range(1, owners):
-        pl.semaphore_signal(
-            barrier, inc=1, device_id={"item": lax.rem(home + step, owners)}, device_id_type=pl.DeviceIdType.MESH
-        )
     items = e_ref.shape[1]
     width = min(items, 8 * LANES)
 
@@ -56,7 +49,7 @@
         values = e_ref[:, columns].astype(jnp.float32)
         parts[0, :, columns] = jnp.sum(values * values, axis=0, keepdims=True)
 
-    pl.semaphore_wait(barrier, n + owners - 2)
+    pl.semaphore_wait(barrier, n - 1)
     copies = []
     for step in range(1, n):
         copy = pltpu.make_async_remote_copy(
@@ -69,76 +62,50 @@
         )
         copy.start()
         copies.append(copy)
-
-    rows = counts.shape[2]
-    high_of = lax.broadcasted_iota(jnp.int32, (owners * rows, width), 0)
-    low_of = lax.broadcasted_iota(jnp.int32, (LANES, width), 0)
-    for level, codes_ref in enumerate((first_ref, second_ref)):
-
-        def add(at, total):
-            codes = codes_ref[:, pl.ds(pl.multiple_of(at * width, width), width)]
-            high = jnp.where(lax.shift_right_logical(codes, 7) == high_of, 1.0, 0.0).astype(jnp.bfloat16)
-            low = jnp.where(lax.bitwise_and(codes, LANES - 1) == low_of, 1.0, 0.0).astype(jnp.bfloat16)
-            return total + lax.dot_general(high, low, (((1,), (1,)), ((), ())), preferred_element_type=jnp.float32)
-
-        total = lax.fori_loop(0, items // width, add, jnp.zeros((owners * rows, LANES), jnp.float32))
-        for owner in range(owners):
-            counts[owner, level] = total[owner * rows:(owner + 1) * rows]
-    for step in range(1, owners):
-        there = lax.rem(home + step, owners)
-        copy = pltpu.make_async_remote_copy(
-            src_ref=counts.at[there],
-            dst_ref=got.at[step],
-            send_sem=send_counts.at[step],
-            recv_sem=recv_counts.at[step],
-            device_id={"item": there},
-            device_id_type=pl.DeviceIdType.MESH,
-        )
-        copy.start()
-        copies.append(copy)
-    for copy in copies[:n - 1]:
+    for copy in copies:
         copy.wait()
     squares = parts[0]
     for step in range(1, n):
         squares = squares + parts[step]
     scale_ref[...] = lax.rsqrt(squares / D + 1e-06)
-    for copy in copies[n - 1:]:
-        copy.wait()
-    held = counts[home]
-    for step in range(1, owners):
-        held = held + got[step]
-    inverse_ref[...] = 0.5 / (held + 1.0)
-
-
-def prepare(embeddings, first_codes, second_codes, n, owners, total):
+
+
+def scales_of(embeddings, n):
     items = embeddings.shape[1]
-    rows = total // owners // LANES
     return pl.pallas_call(
-        functools.partial(prepare_kernel, n, owners),
-        out_shape=(
-            jax.ShapeDtypeStruct((1, items), jnp.float32),
-            jax.ShapeDtypeStruct((2, rows, LANES), jnp.float32),
-        ),
-        in_specs=[VMEM] * 3,
-        out_specs=(VMEM, VMEM),
+        functools.partial(scales_kernel, n),
+        out_shape=jax.ShapeDtypeStruct((1, items), jnp.float32),
+        in_specs=[VMEM],
+        out_specs=VMEM,
         scratch_shapes=[
             pltpu.VMEM((n, 1, items), jnp.float32),
-            pltpu.VMEM((owners, 2, rows, LANES), jnp.float32),
-            pltpu.VMEM((owners, 2, rows, LANES), jnp.float32),
             pltpu.SemaphoreType.DMA((n,)),
             pltpu.SemaphoreType.DMA((n,)),
-            pltpu.SemaphoreType.DMA((owners,)),
-            pltpu.SemaphoreType.DMA((owners,)),
         ],
         compiler_params=pltpu.CompilerParams(collective_id=0, has_side_effects=True, vmem_limit_bytes=VMEM_BYTES),
         cost_estimate=pl.CostEstimate(flops=0, bytes_accessed=16 * MIB, transcendentals=0),
-        name="prepare",
-    )(embeddings, first_codes[None, :], second_codes[None, :])
+        name="scales",
+    )(embeddings)
+
+
+def count_codes(codes_ref, total):
+    items = codes_ref.shape[1]
+    width = min(items, 8 * LANES)
+    high_of = lax.broadcasted_iota(jnp.int32, (total // LANES, width), 0)
+    low_of = lax.broadcasted_iota(jnp.int32, (LANES, width), 0)
+
+    def add(at, held):
+        codes = codes_ref[:, pl.ds(pl.multiple_of(at * width, width), width)]
+        high = jnp.where(lax.shift_right_logical(codes, 7) == high_of, 1.0, 0.0).astype(jnp.bfloat16)
+        low = jnp.where(lax.bitwise_and(codes, LANES - 1) == low_of, 1.0, 0.0).astype(jnp.bfloat16)
+        return held + lax.dot_general(high, low, (((1,), (1,)), ((), ())), preferred_element_type=jnp.float32)
+
+    return lax.fori_loop(0, items // width, add, jnp.zeros((total // LANES, LANES), jnp.float32))
 
 
 def clear(piles):
     rows = piles[0].shape[0]
-    step = min(rows, 64)
+    step = min(rows, 128)
 
     @pl.loop(0, rows // step)
     def _(at):
@@ -148,7 +115,7 @@
 
 def merge(piles):
     rows = piles[0].shape[0]
-    step = min(rows, 64)
+    step = min(rows, 128)
 
     @pl.loop(0, rows // step)
     def _(at):
@@ -167,7 +134,6 @@
     ]
     for at in range(PILES):
         piles[at][pl.ds(codes[at], 1), :] = first[at]
-    for at in range(PILES):
         piles[at][pl.ds(codes[at + PILES], 1), :] = second[at]
 
 
@@ -248,10 +214,15 @@
             out_ref[:, span] = (middle_ref[span, :] - stage[...]).T
 
 
-def exchange_kernel(
-    n, sums_ref, old_ref, inverse_ref, whole_ref, own_ref, old, inverse, fresh, kept, slots,
-    keep_sems, own_sems, send_in, recv_in, send_out, recv_out
-):
+def exchange_kernel(n, counting, sums_ref, old_ref, *refs):
+    if counting:
+        *codes_refs, whole_ref, own_ref, inverse_ref = refs[:5]
+        counts, got, send_counts, recv_counts = refs[-4:]
+        refs = refs[5:-4]
+    else:
+        inverse_ref, whole_ref, own_ref = refs[:3]
+        refs = refs[3:]
+    old, inverse, fresh, kept, slots, keep_sems, own_sems, send_in, recv_in, send_out, recv_out = refs
     levels = n.bit_length() - 1
     me = lax.axis_index("item")
     size = sums_ref.shape[0] // n
@@ -314,13 +285,33 @@
         for path, far in enumerate(fars):
             send(sum_copy(path, 0, far, sums_ref.at[block(flip(me, (0,) + far), path)]))
 
+    def count_copy(step):
+        there = lax.rem(me + step, n)
+        return pltpu.make_async_remote_copy(
+            src_ref=counts.at[there],
+            dst_ref=got.at[step],
+            send_sem=send_counts.at[step],
+            recv_sem=recv_counts.at[step],
+            device_id={"item": there},
+            device_id_type=pl.DeviceIdType.MESH,
+        )
+
+    def spread(level_inverse):
+        for at in range(size // LANES):
+            span = slice(at * LANES, (at + 1) * LANES)
+            inverse[span, :] = jnp.broadcast_to(level_inverse[at:at + 1, :], (old.shape[1], LANES)).T
+
     barrier = pltpu.get_barrier_semaphore()
-    for bit in range(levels):
-        pl.semaphore_signal(barrier, inc=1, device_id={"item": flip(me, [bit])}, device_id_type=pl.DeviceIdType.MESH)
+    if counting:
+        peers = [lax.rem(me + step, n) for step in range(1, n)]
+    else:
+        peers = [flip(me, [bit]) for bit in range(levels)]
+    for peer in peers:
+        pl.semaphore_signal(barrier, inc=1, device_id={"item": peer}, device_id_type=pl.DeviceIdType.MESH)
     for fars in fars_of(0):
         for path, far in enumerate(fars):
             keep_copy(path, far).start()
-    pl.semaphore_wait(barrier, levels)
+    pl.semaphore_wait(barrier, len(peers))
 
     opening = fars_of(0)
     middle = len(opening) // 2
@@ -348,14 +339,33 @@
                 else:
                     rows = pl.ds(path * part, part)
                     fresh[rows, :] = old[rows, :] + total * inverse[rows, :]
-                    for later in range(levels):
-                        send(new_copy(path, later, (), fresh.at[rows], block(me, path)))
+                    send(new_copy(path, 0, (), fresh.at[rows], block(me, path)))
                     pltpu.make_async_copy(fresh.at[rows], whole_ref.at[block(me, path)], own_sems.at[path]).start()
         if step == 0:
             for at in range(size // LANES):
                 span = slice(at * LANES, (at + 1) * LANES)
                 old[span, :] = (0.5 * old_ref[:, span]).T
-                inverse[span, :] = jnp.broadcast_to(inverse_ref[at:at + 1, :], (old.shape[1], LANES)).T
+            if counting:
+                rows = counts.shape[2]
+                for level, codes_ref in enumerate(codes_refs):
+                    held = count_codes(codes_ref, n * size)
+                    for owner in range(n):
+                        counts[owner, level] = held[owner * rows:(owner + 1) * rows]
+                for away in range(1, n):
+                    send(count_copy(away))
+            else:
+                spread(inverse_ref[...])
+        if step == levels - 2 and counting:
+            held = counts[me]
+            for away in range(1, n):
+                count_copy(away).wait_recv()
+                held = held + got[away]
+            both = 0.5 / (held + 1.0)
+            spread(both[0])
+            inverse_ref[...] = both[1]
+    for later in range(1, levels):
+        for path in range(PATHS):
+            send(new_copy(path, later, (), fresh.at[pl.ds(path * part, part)], block(me, path)))
 
     for step in range(levels):
         for helds in zip(*(subsets(order[::-1][:step], (0, 1)) for order in orders)):
@@ -377,35 +387,44 @@
         copy.wait_send()
 
 
-def exchange(sums, old, inverse, n, collective_id):
+def exchange(sums, old, n, collective_id, inverse=None, codes=()):
     rows, width = sums.shape
     size = rows // n
     part = size // PATHS
     count = PATHS * (n - 1)
+    out_shape = [jax.ShapeDtypeStruct(sums.shape, jnp.float32), jax.ShapeDtypeStruct((width, size), jnp.float32)]
+    scratch = [
+        pltpu.VMEM((size, width), jnp.float32),
+        pltpu.VMEM((size, width), jnp.float32),
+        pltpu.VMEM((size, width), jnp.float32),
+        pltpu.VMEM((PATHS * n // 2, part, width), jnp.float32),
+        pltpu.VMEM((count, part, width), jnp.float32),
+        pltpu.SemaphoreType.DMA((PATHS * n // 2,)),
+        pltpu.SemaphoreType.DMA((PATHS,)),
+        pltpu.SemaphoreType.DMA((count,)),
+        pltpu.SemaphoreType.DMA((count,)),
+        pltpu.SemaphoreType.DMA((count,)),
+        pltpu.SemaphoreType.DMA((count,)),
+    ]
+    if codes:
+        inputs = (sums, old) + tuple(level[None, :] for level in codes)
+        out_shape.append(jax.ShapeDtypeStruct((size // LANES, LANES), jnp.float32))
+        scratch += [pltpu.VMEM((n, len(codes), size // LANES, LANES), jnp.float32)] * 2
+        scratch += [pltpu.SemaphoreType.DMA((n,))] * 2
+    else:
+        inputs = (sums, old, inverse)
     return pl.pallas_call(
-        functools.partial(exchange_kernel, n),
-        out_shape=(jax.ShapeDtypeStruct(sums.shape, jnp.float32), jax.ShapeDtypeStruct((width, size), jnp.float32)),
-        in_specs=[ANY, VMEM, VMEM],
-        out_specs=(ANY, VMEM),
-        scratch_shapes=[
-            pltpu.VMEM((size, width), jnp.float32),
-            pltpu.VMEM((size, width), jnp.float32),
-            pltpu.VMEM((size, width), jnp.float32),
-            pltpu.VMEM((PATHS * n // 2, part, width), jnp.float32),
-            pltpu.VMEM((count, part, width), jnp.float32),
-            pltpu.SemaphoreType.DMA((PATHS * n // 2,)),
-            pltpu.SemaphoreType.DMA((PATHS,)),
-            pltpu.SemaphoreType.DMA((count,)),
-            pltpu.SemaphoreType.DMA((count,)),
-            pltpu.SemaphoreType.DMA((count,)),
-            pltpu.SemaphoreType.DMA((count,)),
-        ],
+        functools.partial(exchange_kernel, n, bool(codes)),
+        out_shape=out_shape,
+        in_specs=[ANY] + [VMEM] * (len(inputs) - 1),
+        out_specs=[ANY] + [VMEM] * (len(out_shape) - 1),
+        scratch_shapes=scratch,
         compiler_params=pltpu.CompilerParams(
             collective_id=collective_id, has_side_effects=True, vmem_limit_bytes=VMEM_BYTES
         ),
         cost_estimate=pl.CostEstimate(flops=0, bytes_accessed=128 * MIB, transcendentals=0),
         name="exchange",
-    )(sums, old, inverse)
+    )(*inputs)
 
 
 def on_device(owners, feature_parts, embeddings, first_codes, second_codes, first_old, second_old):
@@ -418,7 +437,7 @@
     row_items = jax.ShapeDtypeStruct((items, width), f32)
 
     stage = pltpu.VMEM((LANES, width), f32)
-    scales, inverse = prepare(embeddings, first_codes, second_codes, feature_parts, owners, total)
+    scales = scales_of(embeddings, feature_parts)
     block = min(items, BLOCK)
     steps = (items // block,)
     local = pltpu.CompilerParams(vmem_limit_bytes=VMEM_BYTES)
@@ -438,7 +457,7 @@
         cost_estimate=cost,
         name="first_sums",
     )(first_codes, embeddings, scales)
-    first_whole, first_own = exchange(first_sums, first_old, inverse[0], owners, 1)
+    first_whole, first_own, inverse = exchange(first_sums, first_old, owners, 1, codes=(first_codes, second_codes))
     middle, second_sums, first_new = pl.pallas_call(
         second_kernel,
         out_shape=(row_items, row_sums, own_shape),
@@ -450,7 +469,7 @@
         cost_estimate=cost,
         name="second_sums",
     )(first_codes, second_codes, normed, first_whole, first_own)
-    second_whole, second_own = exchange(second_sums, second_old, inverse[1], owners, 2)
+    second_whole, second_own = exchange(second_sums, second_old, owners, 2, inverse=inverse)
     leftover, second_new = pl.pallas_call(
         last_kernel,
         out_shape=(jax.ShapeDtypeStruct((width, items), f32), own_shape),

time: 164 us -> 160 us (0.976)
  Pallas kernels: 162 us -> 159 us
    pallas_call x3, Pallas kernels: 101 us -> 98.2 us  [the longest x2 89.2 us: exchange(): pl.pallas_call(functools.partial(exchange_kernel, n, bool(codes)), out_sh...]
where the time goes in v4:
time: 160 us
  Pallas kernels  159 us (99%)
    pallas_call x2, Pallas kernels, exchange(): pl.pallas_call(functools.partial(exchange_kernel, n, bool(codes)), out_sh...  89.2 us
    pallas_call x1, Pallas kernels, on_device(): pl.pallas_call(second_kernel, out_shape=(row_items, row_sums, own_shape),...  25.9 us
    pallas_call x1, Pallas kernels, on_device(): pl.pallas_call(first_kernel, out_shape=(row_items, row_sums), grid=steps,...  20.5 us
    pallas_call x1, Pallas kernels, on_device(): pl.pallas_call(last_kernel, out_shape=(jax.ShapeDtypeStruct((width, items...  14.3 us
    pallas_call x1, Pallas kernels, scales_of(): pl.pallas_call(functools.partial(scales_kernel, n), out_shape=jax.ShapeDt...  9 us

profile of v4, /device:TPU:1, one launch (start us, length us, event | category | flops | bytes accessed | tf_op | source)
XLA Modules:
  0.0 159.6 jit_solution(3631798386350385041)
XLA Ops:
  0.6 9.0 %scales.1.scale_ref = f32[1,8192]{1,0:T(1,128)} custom-call(bf16[128,8192]{1,0:T(8,128)(2,1)} %e_ref.3), custom_call_target="tpu_custom_call" | custom-call | bytes 16777216 | tf_op jit(solution)/shard_map/scales/pallas_call | solution.py:75
  9.6 20.5 %first_sums.1 = (f32[8192,128]{1,0:T(8,128)}, f32[8192,128]{1,0:T(8,128)}) custom-call(s32[8192]{0:T(1024)} %first_ref.1, bf16[128,8192]{1,0:T(8,128)(2,1)} %e_ref.3, f32[1,8192]{1,0:T(1,128)} %scales.1.scale_ref), custom_call_target="tpu_custom_call" | custom-call | bytes 67108864 | tf_op jit(solution)/shard_map/first_sums/pallas_call | solution.py:449
  30.1 46.4 %exchange.2 = (f32[8192,128]{1,0:T(8,128)}, f32[128,1024]{1,0:T(8,128)}, f32[8,128]{1,0:T(8,128)}) custom-call(f32[8192,128]{1,0:T(8,128)} %get-tuple-element.16.sums_ref, f32[128,1024]{1,0:T(8,128)} %old_ref.2, s32[1,8192]{1,0:T(1,128)} %bitcast.2, s32[1,8192]{1,0:T(1,128)} %bitcast.3), custom_call_target="tpu_custom_call" | custom-call | bytes 134217728 | tf_op jit(solution)/shard_map/exchange/pallas_call | solution.py:416
  76.6 25.9 %second_sums.1 = (f32[8192,128]{1,0:T(8,128)}, f32[8192,128]{1,0:T(8,128)}, f32[128,1024]{1,0:T(8,128)}) custom-call(s32[8192]{0:T(1024)} %first_ref.1, s32[8192]{0:T(1024)} %codes_ref.3, f32[8192,128]{1,0:T(8,128)} %get-tuple-element.15.normed_ref, f32[8192,128]{1,0:T(8,128)} %get-tuple-element.17.table_ref, f32[128,1024]{1,0:T(8,128)} %get-tuple-element.18.own_ref), custom_call_target="tpu_custom_call" | custom-call | bytes 67108864 | tf_op jit(solution)/shard_map/second_sums/pallas_call | solution.py:461
  102.5 42.8 %exchange.3 = (f32[8192,128]{1,0:T(8,128)}, f32[128,1024]{1,0:T(8,128)}) custom-call(f32[8192,128]{1,0:T(8,128)} %get-tuple-element.21.sums_ref, f32[128,1024]{1,0:T(8,128)} %old_ref.3, f32[8,128]{1,0:T(8,128)} %get-tuple-element.22.refs_0_), custom_call_target="tpu_custom_call" | custom-call | bytes 134217728 | tf_op jit(solution)/shard_map/exchange/pallas_call | solution.py:416
  145.3 14.3 %leftover.1 = (f32[128,8192]{1,0:T(8,128)}, f32[128,1024]{1,0:T(8,128)}) custom-call(s32[8192]{0:T(1024)} %codes_ref.3, f32[8192,128]{1,0:T(8,128)} %get-tuple-element.20.middle_ref, f32[8192,128]{1,0:T(8,128)} %get-tuple-element.23.table_ref, f32[128,1024]{1,0:T(8,128)} %get-tuple-element.24.own_ref), custom_call_target="tpu_custom_call" | custom-call | bytes 67108864 | tf_op jit(solution)/shard_map/leftover/pallas_call | solution.py:473

commit v5 on v4

--- a/solution.py
+++ b/solution.py
@@ -10,10 +10,13 @@
 
 D = 512
 LANES = 128
-PILES = 8
-GROUP = 2 * PILES
+FIRST_PILES = 4
+FIRST_GROUP = 16
+SECOND_PILES = 8
+SECOND_GROUP = 32
+GROUP = 16
 SPAN = 128
-BLOCK = 1024
+BLOCK = 2048
 PATHS = 4
 MIB = 2**20
 VMEM_BYTES = 56 * MIB
@@ -127,14 +130,15 @@
 
 
 def add_rows(piles, codes, rows):
-    held = [piles[at % PILES][pl.ds(code, 1), :] for at, code in enumerate(codes)]
-    first = [held[at] + rows[at] for at in range(PILES)]
-    second = [
-        jnp.where(codes[at] == codes[at + PILES], first[at], held[at + PILES]) + rows[at + PILES] for at in range(PILES)
-    ]
-    for at in range(PILES):
-        piles[at][pl.ds(codes[at], 1), :] = first[at]
-        piles[at][pl.ds(codes[at + PILES], 1), :] = second[at]
+    held = [piles[at % len(piles)][pl.ds(code, 1), :] for at, code in enumerate(codes)]
+    results = []
+    for at, code in enumerate(codes):
+        value = held[at]
+        for earlier in range(at % len(piles), at, len(piles)):
+            value = jnp.where(code == codes[earlier], results[earlier], value)
+        results.append(value + rows[at])
+    for at, code in enumerate(codes):
+        piles[at % len(piles)][pl.ds(code, 1), :] = results[at]
 
 
 def first_kernel(codes_ref, e_ref, scale_ref, normed_ref, sums_ref, left, right, *more):
@@ -155,9 +159,9 @@
             stage[...] = block
             normed_ref[span, :] = block
         for which, stage in enumerate((left, right)):
-            for start in range(0, LANES, GROUP):
-                rows = [stage[start + j:start + j + 1, :] for j in range(GROUP)]
-                add_rows(piles, [codes_ref[offset + base + which * LANES + start + j] for j in range(GROUP)], rows)
+            for start in range(0, LANES, FIRST_GROUP):
+                rows = [stage[start + j:start + j + 1, :] for j in range(FIRST_GROUP)]
+                add_rows(piles, [codes_ref[offset + base + which * LANES + start + j] for j in range(FIRST_GROUP)], rows)
 
     @pl.when(pl.program_id(0) == pl.num_programs(0) - 1)
     def _():
@@ -176,14 +180,14 @@
 
     @pl.loop(0, items // SPAN)
     def _(at):
-        for start in range(0, SPAN, GROUP):
-            base = pl.multiple_of(at * SPAN + start, GROUP)
+        for start in range(0, SPAN, SECOND_GROUP):
+            base = pl.multiple_of(at * SPAN + start, SECOND_GROUP)
             rows = [
                 normed_ref[pl.ds(base + j, 1), :] - table_ref[pl.ds(first_ref[offset + base + j], 1), :]
-                for j in range(GROUP)
+                for j in range(SECOND_GROUP)
             ]
-            add_rows(piles, [second_ref[offset + base + j] for j in range(GROUP)], rows)
-            for j in range(GROUP):
+            add_rows(piles, [second_ref[offset + base + j] for j in range(SECOND_GROUP)], rows)
+            for j in range(SECOND_GROUP):
                 middle_ref[pl.ds(base + j, 1), :] = rows[j]
 
     @pl.when(pl.program_id(0) == pl.num_programs(0) - 1)
@@ -432,7 +436,7 @@
     total = first_old.shape[1] * owners
     f32 = jnp.float32
     cost = pl.CostEstimate(flops=0, bytes_accessed=64 * MIB, transcendentals=0)
-    piles = [pltpu.VMEM((total, width), f32)] * (PILES - 1)
+    pile = pltpu.VMEM((total, width), f32)
     row_sums = jax.ShapeDtypeStruct((total, width), f32)
     row_items = jax.ShapeDtypeStruct((items, width), f32)
 
@@ -452,7 +456,7 @@
         grid=steps,
         in_specs=[SMEM, by_columns, pl.BlockSpec((1, block), lambda at: (0, at))],
         out_specs=(by_rows, table),
-        scratch_shapes=[stage, stage] + piles,
+        scratch_shapes=[stage, stage] + [pile] * (FIRST_PILES - 1),
         compiler_params=local,
         cost_estimate=cost,
         name="first_sums",
@@ -464,7 +468,7 @@
         grid=steps,
         in_specs=[SMEM, SMEM, by_rows, table, own],
         out_specs=(by_rows, table, own),
-        scratch_shapes=piles,
+        scratch_shapes=[pile] * (SECOND_PILES - 1),
         compiler_params=local,
         cost_estimate=cost,
         name="second_sums",

time: 160 us -> 178 us (1.11)
  Pallas kernels: 159 us -> 178 us
    pallas_call x1, Pallas kernels: 25.9 us -> 39.8 us  [on_device(): pl.pallas_call(second_kernel, out_shape=(row_items, row_sums, own_shape),...]
    pallas_call x1, Pallas kernels: 20.5 us -> 25.1 us  [on_device(): pl.pallas_call(first_kernel, out_shape=(row_items, row_sums), grid=steps,...]
where the time goes in v5:
time: 178 us
  Pallas kernels  178 us (100%)
    pallas_call x2, Pallas kernels, exchange(): pl.pallas_call(functools.partial(exchange_kernel, n, bool(codes)), out_sh...  89.2 us
    pallas_call x1, Pallas kernels, on_device(): pl.pallas_call(second_kernel, out_shape=(row_items, row_sums, own_shape),...  39.8 us
    pallas_call x1, Pallas kernels, on_device(): pl.pallas_call(first_kernel, out_shape=(row_items, row_sums), grid=steps,...  25.1 us
    pallas_call x1, Pallas kernels, on_device(): pl.pallas_call(last_kernel, out_shape=(jax.ShapeDtypeStruct((width, items...  14.4 us
    pallas_call x1, Pallas kernels, scales_of(): pl.pallas_call(functools.partial(scales_kernel, n), out_shape=jax.ShapeDt...  9 us

profile of v5, /device:TPU:1, one launch (start us, length us, event | category | flops | bytes accessed | tf_op | source)
XLA Modules:
  0.0 178.2 jit_solution(5854563573982616859)
XLA Ops:
  0.6 9.0 %scales.1.scale_ref = f32[1,8192]{1,0:T(1,128)} custom-call(bf16[128,8192]{1,0:T(8,128)(2,1)} %e_ref.3), custom_call_target="tpu_custom_call" | custom-call | bytes 16777216 | tf_op jit(solution)/shard_map/scales/pallas_call | solution.py:78
  9.6 25.1 %first_sums.1 = (f32[8192,128]{1,0:T(8,128)}, f32[8192,128]{1,0:T(8,128)}) custom-call(s32[8192]{0:T(1024)} %first_ref.1, bf16[128,8192]{1,0:T(8,128)(2,1)} %e_ref.3, f32[1,8192]{1,0:T(1,128)} %scales.1.scale_ref), custom_call_target="tpu_custom_call" | custom-call | bytes 67108864 | tf_op jit(solution)/shard_map/first_sums/pallas_call | solution.py:453
  34.7 46.4 %exchange.2 = (f32[8192,128]{1,0:T(8,128)}, f32[128,1024]{1,0:T(8,128)}, f32[8,128]{1,0:T(8,128)}) custom-call(f32[8192,128]{1,0:T(8,128)} %get-tuple-element.16.sums_ref, f32[128,1024]{1,0:T(8,128)} %old_ref.2, s32[1,8192]{1,0:T(1,128)} %bitcast.2, s32[1,8192]{1,0:T(1,128)} %bitcast.3), custom_call_target="tpu_custom_call" | custom-call | bytes 134217728 | tf_op jit(solution)/shard_map/exchange/pallas_call | solution.py:420
  81.2 39.8 %second_sums.1 = (f32[8192,128]{1,0:T(8,128)}, f32[8192,128]{1,0:T(8,128)}, f32[128,1024]{1,0:T(8,128)}) custom-call(s32[8192]{0:T(1024)} %first_ref.1, s32[8192]{0:T(1024)} %codes_ref.3, f32[8192,128]{1,0:T(8,128)} %get-tuple-element.15.normed_ref, f32[8192,128]{1,0:T(8,128)} %get-tuple-element.17.table_ref, f32[128,1024]{1,0:T(8,128)} %get-tuple-element.18.own_ref), custom_call_target="tpu_custom_call" | custom-call | bytes 67108864 | tf_op jit(solution)/shard_map/second_sums/pallas_call | solution.py:465
  121.0 42.8 %exchange.3 = (f32[8192,128]{1,0:T(8,128)}, f32[128,1024]{1,0:T(8,128)}) custom-call(f32[8192,128]{1,0:T(8,128)} %get-tuple-element.21.sums_ref, f32[128,1024]{1,0:T(8,128)} %old_ref.3, f32[8,128]{1,0:T(8,128)} %get-tuple-element.22.refs_0_), custom_call_target="tpu_custom_call" | custom-call | bytes 134217728 | tf_op jit(solution)/shard_map/exchange/pallas_call | solution.py:420
  163.8 14.4 %leftover.1 = (f32[128,8192]{1,0:T(8,128)}, f32[128,1024]{1,0:T(8,128)}) custom-call(s32[8192]{0:T(1024)} %codes_ref.3, f32[8192,128]{1,0:T(8,128)} %get-tuple-element.20.middle_ref, f32[8192,128]{1,0:T(8,128)} %get-tuple-element.23.table_ref, f32[128,1024]{1,0:T(8,128)} %get-tuple-element.24.own_ref), custom_call_target="tpu_custom_call" | custom-call | bytes 67108864 | tf_op jit(solution)/shard_map/leftover/pallas_call | solution.py:477

commit v6 on v4

--- a/solution.py
+++ b/solution.py
@@ -11,7 +11,7 @@
 D = 512
 LANES = 128
 PILES = 8
-GROUP = 2 * PILES
+GROUP = PILES
 SPAN = 128
 BLOCK = 1024
 PATHS = 4
@@ -127,14 +127,10 @@
 
 
 def add_rows(piles, codes, rows):
-    held = [piles[at % PILES][pl.ds(code, 1), :] for at, code in enumerate(codes)]
-    first = [held[at] + rows[at] for at in range(PILES)]
-    second = [
-        jnp.where(codes[at] == codes[at + PILES], first[at], held[at + PILES]) + rows[at + PILES] for at in range(PILES)
-    ]
-    for at in range(PILES):
-        piles[at][pl.ds(codes[at], 1), :] = first[at]
-        piles[at][pl.ds(codes[at + PILES], 1), :] = second[at]
+    held = [pile[pl.ds(code, 1), :] for pile, code in zip(piles, codes)]
+    results = [value + row for value, row in zip(held, rows)]
+    for pile, code, result in zip(piles, codes, results):
+        pile[pl.ds(code, 1), :] = result
 
 
 def first_kernel(codes_ref, e_ref, scale_ref, normed_ref, sums_ref, left, right, *more):

time: 160 us -> 152 us (0.950)
  Pallas kernels: 159 us -> 151 us
    pallas_call x1, Pallas kernels: 25.9 us -> 21.4 us  [on_device(): pl.pallas_call(second_kernel, out_shape=(row_items, row_sums, own_shape),...]
    pallas_call x1, Pallas kernels: 20.5 us -> 17.5 us  [on_device(): pl.pallas_call(first_kernel, out_shape=(row_items, row_sums), grid=steps,...]
where the time goes in v6:
time: 152 us
  Pallas kernels  151 us (99%)
    pallas_call x2, Pallas kernels, exchange(): pl.pallas_call(functools.partial(exchange_kernel, n, bool(codes)), out_sh...  89.2 us
    pallas_call x1, Pallas kernels, on_device(): pl.pallas_call(second_kernel, out_shape=(row_items, row_sums, own_shape),...  21.4 us
    pallas_call x1, Pallas kernels, on_device(): pl.pallas_call(first_kernel, out_shape=(row_items, row_sums), grid=steps,...  17.5 us
    pallas_call x1, Pallas kernels, on_device(): pl.pallas_call(last_kernel, out_shape=(jax.ShapeDtypeStruct((width, items...  14.3 us
    pallas_call x1, Pallas kernels, scales_of(): pl.pallas_call(functools.partial(scales_kernel, n), out_shape=jax.ShapeDt...  9 us

profile of v6, /device:TPU:1, one launch (start us, length us, event | category | flops | bytes accessed | tf_op | source)
XLA Modules:
  0.0 152.1 jit_solution(10678421628088310402)
XLA Ops:
  0.6 9.0 %scales.1.scale_ref = f32[1,8192]{1,0:T(1,128)} custom-call(bf16[128,8192]{1,0:T(8,128)(2,1)} %e_ref.3), custom_call_target="tpu_custom_call" | custom-call | bytes 16777216 | tf_op jit(solution)/shard_map/scales/pallas_call | solution.py:75
  9.6 17.5 %first_sums.1 = (f32[8192,128]{1,0:T(8,128)}, f32[8192,128]{1,0:T(8,128)}) custom-call(s32[8192]{0:T(1024)} %first_ref.1, bf16[128,8192]{1,0:T(8,128)(2,1)} %e_ref.3, f32[1,8192]{1,0:T(1,128)} %scales.1.scale_ref), custom_call_target="tpu_custom_call" | custom-call | bytes 67108864 | tf_op jit(solution)/shard_map/first_sums/pallas_call | solution.py:445
  27.2 46.4 %exchange.2 = (f32[8192,128]{1,0:T(8,128)}, f32[128,1024]{1,0:T(8,128)}, f32[8,128]{1,0:T(8,128)}) custom-call(f32[8192,128]{1,0:T(8,128)} %get-tuple-element.16.sums_ref, f32[128,1024]{1,0:T(8,128)} %old_ref.2, s32[1,8192]{1,0:T(1,128)} %bitcast.2, s32[1,8192]{1,0:T(1,128)} %bitcast.3), custom_call_target="tpu_custom_call" | custom-call | bytes 134217728 | tf_op jit(solution)/shard_map/exchange/pallas_call | solution.py:412
  73.6 21.4 %second_sums.1 = (f32[8192,128]{1,0:T(8,128)}, f32[8192,128]{1,0:T(8,128)}, f32[128,1024]{1,0:T(8,128)}) custom-call(s32[8192]{0:T(1024)} %first_ref.1, s32[8192]{0:T(1024)} %codes_ref.3, f32[8192,128]{1,0:T(8,128)} %get-tuple-element.15.normed_ref, f32[8192,128]{1,0:T(8,128)} %get-tuple-element.17.table_ref, f32[128,1024]{1,0:T(8,128)} %get-tuple-element.18.own_ref), custom_call_target="tpu_custom_call" | custom-call | bytes 67108864 | tf_op jit(solution)/shard_map/second_sums/pallas_call | solution.py:457
  95.0 42.8 %exchange.3 = (f32[8192,128]{1,0:T(8,128)}, f32[128,1024]{1,0:T(8,128)}) custom-call(f32[8192,128]{1,0:T(8,128)} %get-tuple-element.21.sums_ref, f32[128,1024]{1,0:T(8,128)} %old_ref.3, f32[8,128]{1,0:T(8,128)} %get-tuple-element.22.refs_0_), custom_call_target="tpu_custom_call" | custom-call | bytes 134217728 | tf_op jit(solution)/shard_map/exchange/pallas_call | solution.py:412
  137.8 14.3 %leftover.1 = (f32[128,8192]{1,0:T(8,128)}, f32[128,1024]{1,0:T(8,128)}) custom-call(s32[8192]{0:T(1024)} %codes_ref.3, f32[8192,128]{1,0:T(8,128)} %get-tuple-element.20.middle_ref, f32[8192,128]{1,0:T(8,128)} %get-tuple-element.23.table_ref, f32[128,1024]{1,0:T(8,128)} %get-tuple-element.24.own_ref), custom_call_target="tpu_custom_call" | custom-call | bytes 67108864 | tf_op jit(solution)/shard_map/leftover/pallas_call | solution.py:469
